TPU v7x, 512 devices: a whole 4x4x16 slice. The times are simulated.
512 devices in a mesh: ia: 8 (over y, core), ja: 8 (over z_lo), al: 8 (over z_hi, x).
Axes of the slice: x: 4, y: 4, z: 16 (z_hi: 2, z_lo: 8; z = z_hi * 8 + z_lo), core: 2. Of those that a mesh axis runs over, the one named last changes fastest.
Arguments:
- text_states: bfloat16 [2048, 8192], P(('ja', 'ia'), 'al'), may hold values from -6 to 6
- latents: bfloat16 [256, 8192], P(('ja', 'ia'), 'al'), may hold values from -6 to 6
- w_query: bfloat16 [8192, 4096], P(('al', 'ja'), 'ia'), may hold values from -0.0625 to 0.0625
- w_key: bfloat16 [8192, 4096], P(('al', 'ja'), 'ia'), may hold values from -0.0625 to 0.0625
- w_value: bfloat16 [8192, 4096], P(('al', 'ja'), 'ia'), may hold values from -0.0625 to 0.0625
- w_output: bfloat16 [4096, 8192], P('ia', ('al', 'ja')), may hold values from -0.09375 to 0.09375
- gate_logit: float32 [8192], P('al'), may hold values from 0.3 to 1.6
- image_index: int32 [2048], P(('ja', 'al')), may hold values from 0 to 3, as said below
- latent_count: int32 [4], replicated, may hold values from 1 to 64, as said below
- grad_output: bfloat16 [2048, 8192], P(('ja', 'ia'), 'al'), may hold values from -6 to 6
Outputs:
- mixed: bfloat16 [2048, 8192], P(('ja', 'ia'), 'al')
- grad_states: bfloat16 [2048, 8192], P(('ja', 'ia'), 'al')
- grad_latents: bfloat16 [256, 8192], P(('ja', 'ia'), 'al')
- grad_w_query: float32 [8192, 4096], P(('al', 'ja'), 'ia')
- grad_w_key: float32 [8192, 4096], P(('al', 'ja'), 'ia')
- grad_w_value: float32 [8192, 4096], P(('al', 'ja'), 'ia')
- grad_w_output: float32 [4096, 8192], P('ia', ('al', 'ja'))
- grad_gate: float32 [8192], P('al')
Inputs may be any that keep to these rules, and one draw needn't show every extreme that they name: `image_index`: image indices never fall along the tokens; token 0 attends image 0 and the last token the last image. `latent_count`: some image has all 64 latents live.
All inputs are finite; a program needn't handle non-finite values.
Results may differ from a plain program's by a relative error of at most 0.035.
Values may be sent and summed in bfloat16 or wider, within the bound.
A program may use at most 64 MiB of HBM per device.

v0:
```python
import math

import jax
import jax.numpy as jnp
from jax import lax
from jax.sharding import PartitionSpec as P

D = 8192
HS = 128
LAT = 64


EPS = 1e-05


def contract_last(left_side, right_side):
    return lax.dot_general(
        left_side, right_side, (((1,), (1,)), ((), ())), preferred_element_type=jnp.float32
    )


def contract_first(left_side, right_side):
    return lax.dot_general(
        left_side, right_side, (((0,), (0,)), ((), ())), preferred_element_type=jnp.float32
    )


def body(
    text_states,
    latents,
    w_query,
    w_key,
    w_value,
    w_output,
    gate_logit,
    image_index,
    latent_count,
    grad_output,
):
    states = text_states.astype(jnp.float32)
    energy = lax.psum(jnp.sum(states * states, axis=1), "al")
    inv_rms = lax.rsqrt(energy / D + EPS)[:, None]
    normed = (states * inv_rms).astype(jnp.bfloat16)
    normed_rows, latent_rows = (
        lax.all_gather(normed, "ia", axis=0, tiled=True),
        lax.all_gather(latents, "ia", axis=0, tiled=True),
    )
    key_all, value_all = (
        lax.all_gather(w_key, "ja", axis=0, tiled=True),
        lax.all_gather(w_value, "ja", axis=0, tiled=True),
    )
    kv_part = jnp.concatenate(
        (
            jnp.dot(latent_rows, key_all, preferred_element_type=jnp.float32),
            jnp.dot(latent_rows, value_all, preferred_element_type=jnp.float32),
        ),
        axis=1,
    )
    kv_total = lax.psum(kv_part.astype(jnp.bfloat16), "al")
    kv_full = lax.all_gather(kv_total, "ja", axis=0, tiled=True)
    width_here = w_query.shape[1]
    columns = normed_rows
    query_part = jnp.dot(
        columns,
        lax.all_gather(w_query, "ja", axis=0, tiled=True),
        preferred_element_type=jnp.float32,
    )
    queries = lax.psum_scatter(
        query_part.astype(jnp.bfloat16), "al", scatter_dimension=0, tiled=True
    )
    rows_here = queries.shape[0]
    heads_here = width_here // HS
    latent_total = kv_full.shape[0]
    key_heads = kv_full[:, :width_here].reshape(latent_total, heads_here, HS)
    value_heads = kv_full[:, width_here:].reshape(latent_total, heads_here, HS)
    query_heads = queries.reshape(rows_here, heads_here, HS)
    latent_slot = jnp.arange(latent_total, dtype=jnp.int32)
    latent_image = latent_slot // LAT
    count_each = jnp.repeat(latent_count, LAT, total_repeat_length=latent_total)
    allowed_pair = (image_index[:, None] == latent_image[None, :]) & (
        (latent_slot % LAT)[None, :] < count_each[None, :]
    )
    score_scale = 1.0 / math.sqrt(HS)
    scores = (
        jnp.einsum("rhd,nhd->rhn", query_heads, key_heads, preferred_element_type=jnp.float32)
        * score_scale
    )
    raised = jnp.where(allowed_pair[:, None, :], jnp.exp(scores), 0.0)
    attend_prob = raised / jnp.sum(raised, axis=2, keepdims=True)
    attend_low = attend_prob.astype(jnp.bfloat16)
    attended = jnp.einsum(
        "rhn,nhd->rhd", attend_low, value_heads, preferred_element_type=jnp.float32
    )
    attended = attended.reshape(rows_here, width_here).astype(jnp.bfloat16)
    attended_rows = lax.all_gather(attended, "al", axis=0, tiled=True)
    output_part = jnp.dot(
        attended_rows,
        lax.all_gather(w_output, "ja", axis=1, tiled=True),
        preferred_element_type=jnp.float32,
    )
    branch_out = lax.psum_scatter(
        output_part.astype(jnp.bfloat16), "ia", scatter_dimension=0, tiled=True
    ).astype(jnp.float32)
    gate_value = jnp.tanh(gate_logit)
    mixed = (states + gate_value * branch_out).astype(jnp.bfloat16)
    upstream = grad_output.astype(jnp.float32)
    grad_gate = lax.psum(
        jnp.sum(upstream * branch_out * (1.0 - gate_value * gate_value), axis=0), ("ia", "ja")
    )
    branch_grad = (upstream * gate_value).astype(jnp.bfloat16)
    branch_rows = lax.all_gather(branch_grad, "ia", axis=0, tiled=True)
    columns = branch_rows
    attended_part = contract_last(columns, lax.all_gather(w_output, "ja", axis=1, tiled=True))
    attended_grad = lax.psum_scatter(
        attended_part.astype(jnp.bfloat16), "al", scatter_dimension=0, tiled=True
    )
    grad_w_output = lax.psum_scatter(
        contract_first(attended_rows, branch_rows).astype(jnp.bfloat16),
        "ja",
        scatter_dimension=1,
        tiled=True,
    ).astype(jnp.float32)
    grad_heads = attended_grad.reshape(rows_here, heads_here, HS)
    prob_grad = jnp.einsum(
        "rhd,nhd->rhn", grad_heads, value_heads, preferred_element_type=jnp.float32
    )
    score_grad = attend_prob * (prob_grad - jnp.sum(attend_prob * prob_grad, axis=2, keepdims=True))
    score_low = score_grad.astype(jnp.bfloat16)
    query_grad = (
        jnp.einsum("rhn,nhd->rhd", score_low, key_heads, preferred_element_type=jnp.float32)
        * score_scale
    )
    query_grad = query_grad.reshape(rows_here, width_here).astype(jnp.bfloat16)
    key_term = (
        jnp.einsum("rhn,rhd->nhd", score_low, query_heads, preferred_element_type=jnp.float32)
        * score_scale
    )
    value_term = jnp.einsum(
        "rhn,rhd->nhd", attend_low, grad_heads, preferred_element_type=jnp.float32
    )
    latent_term = jnp.concatenate(
        (key_term.reshape(latent_total, width_here), value_term.reshape(latent_total, width_here)),
        axis=1,
    )
    latent_grad = lax.psum(latent_term, ("ja", "al")).astype(jnp.bfloat16)
    query_rows = lax.all_gather(query_grad, "al", axis=0, tiled=True)
    grad_w_query = lax.psum_scatter(
        contract_first(normed_rows, query_rows).astype(jnp.bfloat16),
        "ja",
        scatter_dimension=0,
        tiled=True,
    ).astype(jnp.float32)
    product = contract_last(query_rows, lax.all_gather(w_query, "ja", axis=0, tiled=True))
    normed_part = product
    normed_grad = lax.psum_scatter(
        normed_part.astype(jnp.bfloat16), "ia", scatter_dimension=0, tiled=True
    ).astype(jnp.float32)
    inner_sum = lax.psum(jnp.sum(normed_grad * states, axis=1), "al")[:, None]
    cubed = inv_rms * inv_rms * inv_rms
    grad_states = (upstream + inv_rms * normed_grad - states * cubed * inner_sum / D).astype(
        jnp.bfloat16
    )
    block_rows = latent_rows.shape[0]
    ja_index = lax.axis_index("ja")
    block_grad = lax.dynamic_slice_in_dim(latent_grad, ja_index * block_rows, block_rows, 0)
    key_block = block_grad[:, :width_here]
    value_block = block_grad[:, width_here:]
    product = contract_last(
        key_block, lax.all_gather(w_key, "ja", axis=0, tiled=True)
    ) + contract_last(value_block, lax.all_gather(w_value, "ja", axis=0, tiled=True))
    grad_latents = lax.psum_scatter(
        product.astype(jnp.bfloat16), "ia", scatter_dimension=0, tiled=True
    )
    latent_all = lax.all_gather(latent_rows, "ja", axis=0, tiled=True)
    narrow = w_key.shape[0]
    latent_slice = lax.dynamic_slice_in_dim(latent_all, ja_index * narrow, narrow, 1)
    grad_w_key = contract_first(latent_slice, latent_grad[:, :width_here])
    grad_w_value = contract_first(latent_slice, latent_grad[:, width_here:])
    return (
        mixed,
        grad_states,
        grad_latents,
        grad_w_query,
        grad_w_key,
        grad_w_value,
        grad_w_output,
        grad_gate,
    )


def solution(mesh):
    placed = (
        P(("ja", "ia"), "al"),
        P(("ja", "ia"), "al"),
        P(("al", "ja"), "ia"),
        P(("al", "ja"), "ia"),
        P(("al", "ja"), "ia"),
        P("ia", ("al", "ja")),
        P("al"),
        P(("ja", "al")),
        P(),
        P(("ja", "ia"), "al"),
    )
    return jax.shard_map(
        body,
        mesh=mesh,
        in_specs=placed,
        out_specs=(
            P(("ja", "ia"), "al"),
            P(("ja", "ia"), "al"),
            P(("ja", "ia"), "al"),
            P(("al", "ja"), "ia"),
            P(("al", "ja"), "ia"),
            P(("al", "ja"), "ia"),
            P("ia", ("al", "ja")),
            P("al"),
        ),
        check_vma=False,
    )
```

profile of v0, /device:TPU:1, one launch (start us, length us, event | category | flops | bytes accessed | tf_op | source)
XLA Modules:
  0.0 1580.8 jit_solution(15660169899508328048)
XLA Ops:
  10.0 19.7 %all-gather = bf16[8,4,1024]{2,1,0:T(4,128)(2,1)S(1)} all-gather(bf16[1,4,1024]{2,1,0:T(4,128)(2,1)} %bitcast.110), channel_id=1, replica_groups=mesh['ia'=8,'ja'=8,'al'=8] {'ia'}, dimensions={0}, use_global_device_ids=true | all-gather | bytes 73728 | tf_op jit(solution)/shard_map/all_gather | solution.py:46
  32.1 40.8 %psum.36 = f32[32]{0:T(128)S(1)} all-reduce(f32[32]{0:T(128)S(1)} %fusion.24), channel_id=1, replica_groups=mesh['ia'=8,'ja'=8,'al'=8] {'al'}, use_global_device_ids=true, to_apply=%region_2.0 | all-reduce | flops 32 | bytes 256 | tf_op jit(solution)/shard_map/psum | solution.py:41
  73.6 2.6 compare_select_fusion.1
  79.5 17.0 %all_gather.45 = bf16[256,1024]{1,0:T(8,128)(2,1)S(1)} all-gather(bf16[32,1024]{1,0:T(8,128)(2,1)S(1)} %fusion.19), channel_id=1, replica_groups=mesh['ia'=8,'ja'=8,'al'=8] {'ia'}, dimensions={0}, use_global_device_ids=true | all-gather | bytes 589824 | tf_op jit(solution)/shard_map/all_gather | solution.py:111
  97.9 41.9 %all-gather.6.cloned.1.call-done = bf16[1024,512]{1,0:T(8,128)(2,1)} async-done(((bf16[128,512]{1,0:T(8,128)(2,1)}), bf16[1024,512]{1,0:T(8,128)(2,1)}) %all-gather.6.cloned.1.call-update) | async-done | bytes 1048592 | tf_op jit(solution)/shard_map/all_gather | solution.py:49
  142.1 55.0 %all-gather.12.cloned.1.call-done = bf16[512,1024]{1,0:T(8,128)(2,1)} async-done(((bf16[512,128]{1,0:T(8,128)(2,1)}), bf16[512,1024]{1,0:T(8,128)(2,1)}) %all-gather.12.cloned.1.call-update) | async-done | bytes 1048592 | tf_op jit(solution)/shard_map/all_gather | solution.py:98
  197.1 2.4 convolution_convert_fusion.4
  199.7 18.6 %all_gather.41 = bf16[256,1024]{1,0:T(8,128)(2,1)S(1)} all-gather(bf16[32,1024]{1,0:T(8,128)(2,1)S(1)} %fusion.25), channel_id=1, replica_groups=mesh['ia'=8,'ja'=8,'al'=8] {'ia'}, dimensions={0}, use_global_device_ids=true | all-gather | bytes 589824 | tf_op jit(solution)/shard_map/all_gather | solution.py:45
  218.2 42.4 %all-gather.10.cloned.1.call-done = bf16[1024,512]{1,0:T(8,128)(2,1)} async-done(((bf16[128,512]{1,0:T(8,128)(2,1)}), bf16[1024,512]{1,0:T(8,128)(2,1)}) %all-gather.10.cloned.1.call-update) | async-done | bytes 1048592 | tf_op jit(solution)/shard_map/all_gather | solution.py:65
  260.7 2.4 convolution_convert_fusion.5
  263.1 145.3 %all-reduce.5.cloned.1.call-done = bf16[32,1024]{1,0:T(8,128)(2,1)} async-done(((bf16[32,1024]{1,0:T(8,128)(2,1)}), bf16[32,1024]{1,0:T(8,128)(2,1)}) %all-reduce.5.cloned.1.call-update) | async-done | bytes 65552 | tf_op jit(solution)/shard_map/psum | solution.py:59
  408.5 43.1 %all_gather.40 = bf16[256,1024]{1,0:T(8,128)(2,1)S(1)} all-gather(bf16[32,1024]{1,0:T(8,128)(2,1)} %all-reduce.5.cloned.1.call-done), channel_id=1, replica_groups=mesh['ia'=8,'ja'=8,'al'=8] {'ja'}, dimensions={0}, use_global_device_ids=true | all-gather | bytes 589824 | tf_op jit(solution)/shard_map/all_gather | solution.py:60
  451.6 65.1 %reduce-scatter.13.cloned.1.call-done = bf16[32,512]{1,0:T(8,128)(2,1)} async-done(((bf16[256,512]{1,0:T(8,128)(2,1)}), bf16[32,512]{1,0:T(8,128)(2,1)}) %reduce-scatter.13.cloned.1.call-update) | async-done | bytes 32784 | tf_op jit(solution)/shard_map/reduce_scatter | solution.py:114
  517.6 103.6 %reduce-scatter.9.cloned.1.call-done = bf16[32,512]{1,0:T(8,128)(2,1)} async-done(((bf16[256,512]{1,0:T(8,128)(2,1)}), bf16[32,512]{1,0:T(8,128)(2,1)}) %reduce-scatter.9.cloned.1.call-update) | async-done | bytes 32784 | tf_op jit(solution)/shard_map/reduce_scatter | solution.py:68
  622.6 57.0 %all_gather.46 = bf16[256,512]{1,0:T(8,128)(2,1)S(1)} all-gather(bf16[32,512]{1,0:T(8,128)(2,1)S(1)} %bitcast.107), channel_id=1, replica_groups=mesh['ia'=8,'ja'=8,'al'=8] {'al'}, dimensions={0}, use_global_device_ids=true | all-gather | bytes 294912 | tf_op jit(solution)/shard_map/all_gather | solution.py:146
  680.2 464.7 %all-reduce.8 = bf16[256,1024]{0,1:T(8,128)(2,1)} all-reduce(f32[256,1024]{0,1:T(8,128)S(1)} %pad_maximum_fusion), channel_id=1, replica_groups=mesh['ia'=8,'ja'=8,'al'=8] {'ja','al'}, use_global_device_ids=true, to_apply=%region_11.12 | all-reduce | flops 262144 | bytes 1572864 | tf_op jit(solution)/shard_map/psum | solution.py:145
  1146.5 2.2 fusion.3
  1150.3 57.4 %all_gather.43 = bf16[256,512]{1,0:T(8,128)(2,1)S(1)} all-gather(bf16[32,512]{1,0:T(8,128)(2,1)S(1)} %bitcast.108), channel_id=1, replica_groups=mesh['ia'=8,'ja'=8,'al'=8] {'al'}, dimensions={0}, use_global_device_ids=true | all-gather | bytes 294912 | tf_op jit(solution)/shard_map/all_gather | solution.py:95
  1214.4 42.0 %all_gather.47 = bf16[256,1024]{1,0:T(8,128)(2,1)S(1)} all-gather(bf16[32,1024]{1,0:T(8,128)(2,1)S(1)} %copy-done.8), channel_id=1, replica_groups=mesh['ia'=8,'ja'=8,'al'=8] {'ja'}, dimensions={0}, use_global_device_ids=true | all-gather | bytes 589824 | tf_op jit(solution)/shard_map/all_gather | solution.py:174
  1258.3 33.9 %all-reduce.7.cloned.1.call-done = bf16[32,1024]{1,0:T(8,128)(2,1)} async-done(((bf16[32,1024]{1,0:T(8,128)(2,1)}), bf16[32,1024]{1,0:T(8,128)(2,1)}) %all-reduce.7.cloned.1.call-update) | async-done | bytes 65552
  1293.5 39.5 %reduce-scatter.15.cloned.1.call-done = bf16[32,1024]{1,0:T(8,128)(2,1)} async-done(((bf16[256,1024]{1,0:T(8,128)(2,1)}), bf16[32,1024]{1,0:T(8,128)(2,1)}) %reduce-scatter.15.cloned.1.call-update) | async-done | bytes 65552 | tf_op jit(solution)/shard_map/reduce_scatter | solution.py:155
  1333.9 41.6 %psum.37 = f32[32]{0:T(128)S(1)} all-reduce(f32[32]{0:T(128)S(1)} %fusion.29), channel_id=1, replica_groups=mesh['ia'=8,'ja'=8,'al'=8] {'al'}, use_global_device_ids=true, to_apply=%region_10.11 | all-reduce | flops 32 | bytes 256 | tf_op jit(solution)/shard_map/psum | solution.py:158
  1377.1 193.4 %psum.39 = f32[1024]{0:T(1024)} all-reduce(f32[1024]{0:T(1024)S(1)} %get-tuple-element.22), channel_id=1, replica_groups=mesh['ia'=8,'ja'=8,'al'=8] {'ia','ja'}, use_global_device_ids=true, to_apply=%region_16.17 | all-reduce | flops 1024 | bytes 8192 | tf_op jit(solution)/shard_map/psum | solution.py:107
  1572.3 1.6 convert_element_type.102
  (96 shorter events, 32.6 us)
Async XLA Ops:
  7.2 89.3 %all-gather.8.cloned.1.call-start = ((), (), s32[]{:S(2)}) async-start(), calls=%async_computation.7 | async-start | bytes 1179648 | tf_op jit(solution)/shard_map/all_gather | solution.py:50
  7.9 131.9 %all-gather.6.cloned.1.call-start = ((), (), s32[]{:S(2)}) async-start(), calls=%async_computation.6 | async-start | bytes 1179648 | tf_op jit(solution)/shard_map/all_gather | solution.py:49
  8.7 188.4 %all-gather.12.cloned.1.call-start = ((), (), s32[]{:S(2)}) async-start(), calls=%async_computation.11 | async-start | bytes 1179648 | tf_op jit(solution)/shard_map/all_gather | solution.py:98
  9.4 251.3 %all-gather.10.cloned.1.call-start = ((), (), s32[]{:S(2)}) async-start(), calls=%async_computation.9 | async-start | bytes 1179648 | tf_op jit(solution)/shard_map/all_gather | solution.py:65
  10.0 398.5 %all-reduce.5.cloned.1.call-start = ((), (), s32[]{:S(2)}) async-start(), calls=%async_computation.8 | async-start | bytes 131072 | tf_op jit(solution)/shard_map/psum | solution.py:59
  29.7 110.1 %copy-start.7 = (bf16[32,1024]{1,0:T(8,128)(2,1)}, bf16[32,1024]{1,0:T(8,128)(2,1)S(1)}, u32[]{:S(2)}) copy-start(bf16[32,1024]{1,0:T(8,128)(2,1)S(1)} %reshape.233) | copy-start | bytes 196612
  142.0 57.6 %copy-start.13 = (s32[32]{0:T(128)S(1)}, s32[32]{0:T(128)}, u32[]{:S(2)}) copy-start(s32[32]{0:T(128)} %param.19) | copy-start | bytes 388
  142.0 374.7 %reduce-scatter.13.cloned.1.call-start = ((), (), s32[]{:S(2)}) async-start(), calls=%async_computation.13 | async-start | bytes 294912 | tf_op jit(solution)/shard_map/reduce_scatter | solution.py:114
  199.5 421.7 %reduce-scatter.9.cloned.1.call-start = ((), (), s32[]{:S(2)}) async-start(), calls=%async_computation.10 | async-start | bytes 294912 | tf_op jit(solution)/shard_map/reduce_scatter | solution.py:68
  263.1 1029.1 %all-reduce.7.cloned.1.call-start = ((), (), s32[]{:S(2)}) async-start(), calls=%async_computation.17 | async-start | bytes 131072
  451.6 171.0 %copy-start.5 = (bf16[32,4,8,128]{3,2,1,0:T(8,128)(2,1)}, bf16[32,4,8,128]{3,2,1,0:T(8,128)(2,1)S(1)}, u32[]{:S(2)}) copy-start(bf16[32,4,8,128]{3,2,1,0:T(8,128)(2,1)S(1)} %get-tuple-element.21) | copy-start | bytes 786436
  517.6 162.0 %copy-start.11 = (bf16[32,512]{1,0:T(8,128)(2,1)S(1)}, bf16[32,512]{1,0:T(8,128)(2,1)}, u32[]{:S(2)}) copy-start(bf16[32,512]{1,0:T(8,128)(2,1)} %reduce-scatter.13.cloned.1.call-done) | copy-start | bytes 98308
  622.3 57.6 %copy-start.12 = (bf16[32,512]{1,0:T(8,128)(2,1)S(1)}, bf16[32,512]{1,0:T(8,128)(2,1)}, u32[]{:S(2)}) copy-start(bf16[32,512]{1,0:T(8,128)(2,1)} %reduce-scatter.9.cloned.1.call-done) | copy-start | bytes 98308
  680.2 464.8 %copy-start.3 = (bf16[1024,512]{1,0:T(8,128)(2,1)S(1)}, bf16[1024,512]{1,0:T(8,128)(2,1)}, u32[]{:S(2)}) copy-start(bf16[1024,512]{1,0:T(8,128)(2,1)} %all-gather.6.cloned.1.call-done) | copy-start | bytes 3145732
  1146.5 2.3 copy-start.1
  1148.7 184.2 %reduce-scatter.15.cloned.1.call-start = ((), (), s32[]{:S(2)}) async-start(), calls=%async_computation.14 | async-start | bytes 589824 | tf_op jit(solution)/shard_map/reduce_scatter | solution.py:155
  1150.1 57.6 %copy-start = (bf16[512,1024]{1,0:T(8,128)(2,1)S(1)}, bf16[512,1024]{1,0:T(8,128)(2,1)}, u32[]{:S(2)}) copy-start(bf16[512,1024]{1,0:T(8,128)(2,1)} %all-gather.12.cloned.1.call-done) | copy-start | bytes 3145732
  1150.1 225.4 %reduce-scatter.11.cloned.1.call-start = ((), (), s32[]{:S(2)}) async-start(), calls=%async_computation.12 | async-start | bytes 589824 | tf_op jit(solution)/shard_map/reduce_scatter | solution.py:101
  1209.0 361.6 %reduce-scatter.19.cloned.1.call-start = ((), (), s32[]{:S(2)}) async-start(), calls=%async_computation.16 | async-start | bytes 1179648
  1210.9 3.5 copy-start.8
  1210.9 361.4 %reduce-scatter.17.cloned.1.call-start = ((), (), s32[]{:S(2)}) async-start(), calls=%async_computation.15 | async-start | bytes 1179648 | tf_op jit(solution)/shard_map/reduce_scatter | solution.py:147
  1212.4 44.0 %copy-start.4 = (bf16[256,1024]{0,1:T(8,128)(2,1)S(1)}, bf16[256,1024]{0,1:T(8,128)(2,1)}, u32[]{:S(2)}) copy-start(bf16[256,1024]{0,1:T(8,128)(2,1)} %all-reduce.8) | copy-start | bytes 1572868
  1212.4 120.6 %copy-start.9 = (bf16[32,1024]{1,0:T(8,128)(2,1)S(1)}, bf16[32,1024]{1,0:T(8,128)(2,1)}, u32[]{:S(2)}) copy-start(bf16[32,1024]{1,0:T(8,128)(2,1)} %param.12) | copy-start | bytes 196612
  1212.4 163.1 %copy-start.10 = (bf16[32,1024]{1,0:T(8,128)(2,1)S(1)}, bf16[32,1024]{1,0:T(8,128)(2,1)}, u32[]{:S(2)}) copy-start(bf16[32,1024]{1,0:T(8,128)(2,1)} %param.21) | copy-start | bytes 196612
  (2 other events, 2.9 us)
Sparse Core Ops, SparseCore 0:
  10.1 66.7 all-gather.7
  78.9 60.8 all-gather.5
  141.8 55.2 all-gather.11
  199.0 61.6 all-gather.9
  264.0 144.4 all-reduce.4
  414.0 102.6 reduce-scatter.12
  521.7 99.4 reduce-scatter.8
  1148.8 143.2 all-reduce.6
  1295.0 37.9 reduce-scatter.14
  1335.8 37.6 reduce-scatter.10
  1376.4 62.3 reduce-scatter.18
  1441.4 61.4 reduce-scatter.16
where the time goes:
time: 1610 us; the launch traced here: 1580 us
  blocking collectives  995 us (62%)
  waiting for transfers between devices  529 us (33%)
  matrix products  20.6 us (1%)
    psum x1, blocking collectives, body(): latent_grad = lax.psum(latent_term, ('ja', 'al')).astype(jnp.bfloat16)  465 us
    psum x1, blocking collectives, body(): lax.psum(jnp.sum(upstream * branch_out * (1.0 - gate_value * gate_value),...  193 us
    psum x1, waiting for transfers between devices, body(): kv_total = lax.psum(kv_part.astype(jnp.bfloat16), 'al')  145 us
    reduce_scatter x1, waiting for transfers between devices, body(): lax.psum_scatter(query_part.astype(jnp.bfloat16), 'al', scatter_dimension...  104 us
    reduce_scatter x1, waiting for transfers between devices, body(): lax.psum_scatter(attended_part.astype(jnp.bfloat16), 'al', scatter_dimens...  65.1 us
    all_gather x1, blocking collectives, body(): attended_rows = lax.all_gather(attended, 'al', axis=0, tiled=True)  57.4 us
    all_gather x1, blocking collectives, body(): query_rows = lax.all_gather(query_grad, 'al', axis=0, tiled=True)  57 us
    all_gather x1, waiting for transfers between devices, body(): lax.all_gather(w_output, 'ja', axis=1, tiled=True)  55 us
  transfers between devices with their start and end apart: 12, of which 8 were waited for; matrix products, arithmetic and copies ran while one was open for 2% of the time, Pallas kernels for 0%

commit v1 on v0

v1 whole, which is shorter than its diff:
```python
import functools
import math

import jax
import jax.numpy as jnp
from jax import lax
from jax.experimental import pallas as pl
from jax.experimental.pallas import tpu as pltpu
from jax.sharding import PartitionSpec as P

MESH = pl.DeviceIdType.MESH
D = 8192
EPS = 1e-05
BF = jnp.bfloat16
F32 = jnp.float32
IMGS = 4
HS = 128
CH = 2


def dot(a, b, ca, cb):
    return lax.dot_general(a, b, (((ca,), (cb,)), ((), ())), preferred_element_type=F32)


def loop(lo, hi, f):
    lax.fori_loop(lo, hi, lambda i, c: (f(i), c)[1], 0)


def kernel(sizes, feats, *refs):
    NI, NJ, NZ, NX = sizes
    (
        st_ref, lat_ref, wq_ref, wk_ref, wv_ref, wo_ref, gate_ref, img_ref, cnt_ref, up_ref,
        mixed_ref, gst_ref, glat_ref, gwq_ref, gwk_ref, gwv_ref, gwo_ref, gg_ref,
    ) = refs[:18]
    sc = list(refs[18:])
    (
        W, strow, brrow, latg, latc, latb, latt,
        kv_p, kv_rx, kv_zs, kv_rz, kv_js, kv_rj, kv_full,
        lg_p, lg_rx, lg_zs, lg_rz, lg_js, lg_rj, lg_full,
        q_p, q_rx, q_zs, q_rz, qs,
        a_p, a_rx, a_zs, a_rz, gs,
        e_p, e_rx, e_zs, e_rz,
        atrow, qgrow, innr, rin,
        outp, outr, normp, normr,
        gg_p, gg_r, ggj, ggj_r,
        gp, grr, grl,
        gl, glr, gls, glf,
        prob, probl,
        ssem, rsem,
    ) = sc
    NA = NZ * NX
    TB, DL = st_ref.shape
    WD = wq_ref.shape[1]
    WB = wq_ref.shape[0]
    HL = WD // HS
    LR = lat_ref.shape[0]
    LI = NI * LR
    NL = NJ * LI
    LB = NL // NA
    LAT = NL // IMGS
    CB = 2 * HL
    TR = NI * TB
    scale = 1.0 / math.sqrt(HS)

    ia, ja, al = lax.axis_index("ia"), lax.axis_index("ja"), lax.axis_index("al")
    x, zh = al % NX, al // NX
    me = {"ia": ia, "ja": ja, "al": al}
    size = {"ia": NI, "ja": NJ}
    zdev = {"al": (1 - zh) * NX + x}
    zal = (1 - zh) * NX + x

    used = [0]

    def take(n):
        used[0] += n
        assert used[0] <= ssem.shape[0]
        return used[0] - n

    drains = []

    def copy(src, dst, i, dev):
        return pltpu.make_async_remote_copy(
            src_ref=src, dst_ref=dst, send_sem=ssem.at[i], recv_sem=rsem.at[i],
            device_id=dev, device_id_type=MESH,
        )

    class Exchange:
        def __init__(self, axis, src, dst):
            self.axis, self.src, self.dst = axis, src, dst
            self.n = NX if axis == "x" else size[axis]
            self.base = take(self.n)
            self.me = x if axis == "x" else me[axis]

        def one(self, k, sending):
            peer = (self.me + k) % self.n if sending else (self.me - k + self.n) % self.n
            dev = {"al": zh * NX + peer} if self.axis == "x" else {self.axis: peer}
            if sending:
                return copy(self.src(peer), self.dst(self.me, k), self.base + k, dev)
            return copy(self.src(peer), self.dst(peer, k), self.base + k, dev)

        def start(self):
            loop(1, self.n, lambda k: self.one(k, True).start())
            drains.append(lambda: loop(1, self.n, lambda k: self.one(k, True).wait_send()))

        def wait(self):
            loop(1, self.n, lambda k: self.one(k, False).wait_recv())

    class Swap:
        def __init__(self, src, dst, landed):
            self.i = take(1)
            self.c = copy(src, dst, self.i, zdev)
            self.r = copy(src, landed, self.i, zdev)

        def start(self):
            if NZ == 2:
                self.c.start()
                drains.append(lambda: self.c.wait_send())

        def wait(self):
            if NZ == 2:
                self.r.wait_recv()

    class Scatter:
        def __init__(self, p, rx, zs, rz):
            self.p, self.rx, self.zs, self.rz = p, rx, zs, rz
            self.ex = Exchange("x", lambda peer: p.at[peer], lambda s, k: rx.at[k])
            self.sw = Swap(zs.at[1 - zh] if NZ == 2 else zs.at[0], rz, rz)

        def s1(self):
            self.ex.start()

        def s2(self):
            self.ex.wait()
            t = self.p[x].astype(F32)
            for k in range(1, NX):
                t = t + self.rx[k].astype(F32)
            self.zs[...] = t.astype(self.zs.dtype)
            self.sw.start()

        def s3(self):
            self.sw.wait()
            t = self.zs[zh].astype(F32)
            if NZ == 2:
                t = t + self.rz[...].astype(F32)
            return t

    class Gather:
        def __init__(self, buf):
            self.sw = Swap(buf.at[al], buf.at[al], buf.at[zal])
            self.e1 = Exchange("x", lambda peer: buf.at[al], lambda s, k: buf.at[zh * NX + s])
            self.e2 = Exchange("x", lambda peer: buf.at[zal], lambda s, k: buf.at[(1 - zh) * NX + s])

        def s1(self):
            self.sw.start()
            self.e1.start()

        def s2(self):
            if NZ == 2:
                self.sw.wait()
                self.e2.start()

        def s3(self):
            self.e1.wait()
            if NZ == 2:
                self.e2.wait()

    class AllSum:
        def __init__(self, p, rx, zs, rz, js, rj, full):
            self.sct = Scatter(p, rx, zs, rz)
            self.js, self.rj, self.full = js, rj, full
            self.ex = Exchange("ja", lambda peer: js.at[peer], lambda s, k: rj.at[k])
            self.ag = Exchange("ja", lambda peer: full.at[al, ja], lambda s, k: full.at[al, s])
            self.gat = Gather(full)

        def s1(self):
            self.sct.s1()

        def s2(self):
            self.sct.s2()

        def s3(self):
            self.js[...] = self.sct.s3().astype(BF)
            self.ex.start()

        def s4(self):
            self.ex.wait()
            t = self.js[ja].astype(F32)
            for k in range(1, NJ):
                t = t + self.rj[k].astype(F32)
            self.full[al, ja] = t.astype(BF)
            self.ag.start()

        def s5(self):
            self.ag.wait()
            self.gat.s1()

        def s6(self):
            self.gat.s2()

        def s7(self):
            self.gat.s3()

    T = NJ * CH
    WR, WL = take(2 * T), take(2 * T)
    nr, nl = (ja + 1) * CH, (NJ - ja) * CH

    def item_right(t):
        m, r = t // nr, t % nr
        return m, r, ja - r // CH, r % CH

    def item_left(t):
        m, r = t // nl, t % nl
        return m, r, ja + r // CH, r % CH

    def line_copy(base, m, s, c, to):
        piece = W.at[m, s, c]
        return copy(piece, piece, base + (m * NJ + s) * CH + c, {"ja": to})

    def line_step(t):
        @pl.when(t < 2 * nr)
        def _():
            m, r, s, c = item_right(t)

            @pl.when(r >= CH)
            def _():
                line_copy(WR, m, s, c, ja - 1).wait_recv()

            @pl.when(ja < NJ - 1)
            def _():
                line_copy(WR, m, s, c, ja + 1).start()

        @pl.when(t < 2 * nl)
        def _():
            m, r, s, c = item_left(t)

            @pl.when(r >= CH)
            def _():
                line_copy(WL, m, s, c, ja + 1).wait_recv()

            @pl.when(ja > 0)
            def _():
                line_copy(WL, m, s, c, ja - 1).start()

    def line_drain(t):
        @pl.when((t < 2 * nr) & (ja < NJ - 1))
        def _():
            m, r, s, c = item_right(t)
            line_copy(WR, m, s, c, ja + 1).wait_send()

        @pl.when((t < 2 * nl) & (ja > 0))
        def _():
            m, r, s, c = item_left(t)
            line_copy(WL, m, s, c, ja - 1).wait_send()

    drains.append(lambda: loop(0, 2 * T, line_drain))

    def line(lo, hi):
        loop(lo * CH, hi * CH, line_step)

    SR, SL = take(2 * NJ), take(2 * NJ)

    def sum_copy(base, buf, m, d, to, src=None):
        return copy(buf.at[m, d] if src is None else src, buf.at[m, d], base + m * NJ + d, {"ja": to})

    def sum_step(m, t):
        @pl.when((t >= ja) & (t < NJ - 1))
        def _():
            d = NJ - 1 - t + ja

            @pl.when(ja == 0)
            def _():
                sum_copy(SR, grr, m, d, ja + 1, gp.at[m, d]).start()

            @pl.when(ja > 0)
            def _():
                sum_copy(SR, grr, m, d, ja - 1).wait_recv()
                grr[m, d] = (grr[m, d].astype(F32) + gp[m, d].astype(F32)).astype(BF)
                sum_copy(SR, grr, m, d, ja + 1).start()

        @pl.when((t >= NJ - 1 - ja) & (t < NJ - 1))
        def _():
            d = t - (NJ - 1 - ja)

            @pl.when(ja == NJ - 1)
            def _():
                sum_copy(SL, grl, m, d, ja - 1, gp.at[m, d]).start()

            @pl.when(ja < NJ - 1)
            def _():
                sum_copy(SL, grl, m, d, ja + 1).wait_recv()
                grl[m, d] = (grl[m, d].astype(F32) + gp[m, d].astype(F32)).astype(BF)
                sum_copy(SL, grl, m, d, ja - 1).start()

    def sum_drain(m, t):
        @pl.when((t >= ja) & (t < NJ - 1))
        def _():
            d = NJ - 1 - t + ja
            sum_copy(SR, grr, m, d, ja + 1).wait_send()

        @pl.when((t >= NJ - 1 - ja) & (t < NJ - 1))
        def _():
            d = t - (NJ - 1 - ja)
            sum_copy(SL, grl, m, d, ja - 1).wait_send()

    def sum_line(m, lo, hi):
        loop(lo, hi, lambda t: sum_step(m, t))

    def sum_end(m):
        t = gp[m, ja].astype(F32)

        @pl.when(ja > 0)
        def _():
            sum_copy(SR, grr, m, ja, ja - 1).wait_recv()

        @pl.when(ja < NJ - 1)
        def _():
            sum_copy(SL, grl, m, ja, ja + 1).wait_recv()

        t = t + jnp.where(ja > 0, grr[m, ja].astype(F32), 0.0)
        t = t + jnp.where(ja < NJ - 1, grl[m, ja].astype(F32), 0.0)
        drains.append(lambda: loop(0, NJ, lambda t: sum_drain(m, t)))
        return t

    ex_lat = Exchange("ia", lambda peer: latg.at[ia], lambda s, k: latg.at[s])
    ex_l2 = Exchange("ja", lambda peer: latc.at[peer], lambda s, k: latb.at[s])
    ex_st = Exchange("ia", lambda peer: strow.at[ia], lambda s, k: strow.at[s])
    ex_br = Exchange("ia", lambda peer: brrow.at[ia], lambda s, k: brrow.at[s])
    kv = AllSum(kv_p, kv_rx, kv_zs, kv_rz, kv_js, kv_rj, kv_full)
    lg = AllSum(lg_p, lg_rx, lg_zs, lg_rz, lg_js, lg_rj, lg_full)
    q_s = Scatter(q_p, q_rx, q_zs, q_rz)
    a_s = Scatter(a_p, a_rx, a_zs, a_rz)
    e_ex = Exchange("x", lambda peer: e_p, lambda s, k: e_rx.at[k])
    e_sw = Swap(e_zs, e_rz, e_rz)
    at_g, qg_g, in_g = Gather(atrow), Gather(qgrow), Gather(innr)
    ex_out = Exchange("ia", lambda peer: outp.at[peer], lambda s, k: outr.at[k])
    ex_norm = Exchange("ia", lambda peer: normp.at[peer], lambda s, k: normr.at[k])
    ex_in = Exchange("ia", lambda peer: innr.at[peer], lambda s, k: rin.at[k])
    ex_gi = Exchange("ia", lambda peer: gg_p, lambda s, k: gg_r.at[k])
    ex_gj = Exchange("ja", lambda peer: ggj, lambda s, k: ggj_r.at[k])
    ex_gl = Exchange("ia", lambda peer: gl.at[peer], lambda s, k: glr.at[k])
    ex_g2 = Exchange("ja", lambda peer: gls.at[peer], lambda s, k: glf.at[s])

    barrier = pltpu.get_barrier_semaphore()
    loop(1, NI, lambda k: pl.semaphore_signal(barrier, 1, device_id={"ia": (ia + k) % NI}, device_id_type=MESH))
    loop(1, NJ, lambda k: pl.semaphore_signal(barrier, 1, device_id={"ja": (ja + k) % NJ}, device_id_type=MESH))
    loop(1, NX, lambda k: pl.semaphore_signal(barrier, 1, device_id={"al": zh * NX + (x + k) % NX}, device_id_type=MESH))
    if NZ == 2:
        pl.semaphore_signal(barrier, 1, device_id=zdev, device_id_type=MESH)
    W[0, ja] = wq_ref[...].reshape(CH, WB // CH, WD)
    strow[ia] = st_ref[...]
    latg[ia] = jnp.zeros((16, DL), BF)
    latg[ia, 0:LR, :] = lat_ref[...]
    gate = jnp.tanh(gate_ref[...])
    brrow[ia] = (up_ref[...].astype(F32) * gate).astype(BF)
    pl.semaphore_wait(barrier, NI - 1 + NJ - 1 + NX - 1 + NZ - 1)

    ex_lat.start()
    line(0, 1)
    ex_st.start()
    W[1, ja] = wo_ref[...].T.reshape(CH, WB // CH, WD)
    ex_br.start()
    line(1, 2)

    ex_lat.wait()
    pick_r = lax.broadcasted_iota(jnp.int32, (LI, NI * 16), 0)
    pick_c = lax.broadcasted_iota(jnp.int32, (LI, NI * 16), 1)
    pick = (pick_c == (pick_r // LR) * 16 + pick_r % LR).astype(F32).astype(BF)
    packed = dot(pick, latg[...].reshape(NI * 16, DL), 1, 0).astype(BF)
    for s in range(NJ):
        latc[s] = packed[:, s * 128 : (s + 1) * 128]
    latb[ja] = latc[ja]
    ex_l2.start()
    line(2, 3)

    ex_l2.wait()
    lat = latb[...].reshape(NL, 128)
    latt[...] = lat.T
    for h in range(CB):
        wref = wk_ref if h < HL else wv_ref
        c = h % HL
        part = dot(lat, wref[:, c * HS : (c + 1) * HS], 1, 0).astype(BF)
        for a in range(NA):
            kv_p[a % NX, a // NX, h] = part[a * LB : (a + 1) * LB]
    kv.s1()
    line(3, 4)

    ex_st.wait()
    states_rows = strow[...].reshape(TR, DL)
    sq = states_rows.astype(F32)
    sq = (sq * sq).astype(BF)
    e_p[...] = dot(jnp.ones((8, DL), BF), sq, 1, 1)[0:1]
    e_ex.start()
    kv.s2()
    line(4, 5)
    kv.s3()
    e_ex.wait()
    t = e_p[...]
    for k in range(1, NX):
        t = t + e_rx[k]
    e_zs[...] = t
    e_sw.start()
    line(5, 6)
    kv.s4()
    line(6, 7)
    kv.s5()
    line(7, 8)
    kv.s6()

    def rows_times(rows, m, p):
        acc = dot(rows, W[m].reshape(DL, WD), 1, 0).astype(BF)
        for a in range(NA):
            p[a % NX, a // NX] = acc[a * TB : (a + 1) * TB]

    rows_times(states_rows, 0, q_p)
    q_s.s1()
    line(8, 9)
    q_s.s2()
    e_sw.wait()
    energy = e_zs[...]
    if NZ == 2:
        energy = energy + e_rz[...]
    inv_row = lax.rsqrt(energy / D + EPS)

    lane = lax.broadcasted_iota(jnp.int32, (TB, TR), 1)
    sub = lax.broadcasted_iota(jnp.int32, (TB, TR), 0)

    def column(block):
        return jnp.sum(jnp.where(lane == block * TB + sub, inv_row, 0.0), axis=1, keepdims=True)

    inv_attn, inv_own = column(al), column(ia)
    line(9, 10)
    kv.s7()
    q = q_s.s3() * inv_attn
    qs[...] = q.astype(BF)

    slot = lax.broadcasted_iota(jnp.int32, (TB, NL), 1)
    image = slot // LAT
    count = jnp.where(image == 0, cnt_ref[0], jnp.where(image == 1, cnt_ref[1], jnp.where(image == 2, cnt_ref[2], cnt_ref[3])))
    allowed = (img_ref[...] == image) & (slot % LAT < count)
    for h in range(HL):
        cols = slice(h * HS, (h + 1) * HS)
        kh = kv_full[:, h].reshape(NL, HS)
        vh = kv_full[:, HL + h].reshape(NL, HS)
        sco = dot(qs[:, cols], kh, 1, 1) * scale
        raised = jnp.where(allowed, jnp.exp(sco), 0.0)
        pr = raised / jnp.sum(raised, axis=1, keepdims=True)
        prob[h] = pr
        probl[h] = pr.astype(BF)
        atrow[al, :, cols] = dot(probl[h], vh, 1, 0).astype(BF)
    at_g.s1()
    line(10, 11)
    at_g.s2()
    ex_br.wait()
    branch_rows = brrow[...].reshape(TR, DL)
    line(11, 16 if NJ == 8 else 2 * NJ)

    def times_rows_t(rows, m, dst):
        for s in range(NJ):
            r = dot(rows, W[m, s].reshape(WB, WD), 1, 1).astype(BF)
            dst[:, :, s * WB : (s + 1) * WB] = r.reshape(NI, TB, WB)

    def grad_parts(left, right, m):
        for s in range(NJ):
            gp[m, s] = dot(left[:, s * WB : (s + 1) * WB], right, 0, 0).astype(BF)

    rows_times(branch_rows, 1, a_p)
    a_s.s1()
    at_g.s3()
    attn_rows = atrow[...].reshape(TR, WD)
    grad_parts(branch_rows, attn_rows, 1)
    sum_line(1, 0, 1)
    a_s.s2()
    times_rows_t(attn_rows, 1, outp)
    ex_out.start()
    sum_line(1, 1, 2)

    grads = a_s.s3()
    gs[...] = grads.astype(BF)
    inner = jnp.zeros((TB, 1), F32)
    for h in range(HL):
        cols = slice(h * HS, (h + 1) * HS)
        kh = kv_full[:, h].reshape(NL, HS)
        vh = kv_full[:, HL + h].reshape(NL, HS)
        gh = gs[:, cols]
        qh = qs[:, cols]
        pg = dot(gh, vh, 1, 1)
        pr = prob[h]
        sg = pr * (pg - jnp.sum(pr * pg, axis=1, keepdims=True))
        sl = sg.astype(BF)
        qg = dot(sl, kh, 1, 0) * scale * inv_attn
        inner = inner + jnp.sum(qg * qh.astype(F32), axis=1, keepdims=True)
        qgrow[al, :, cols] = qg.astype(BF)
        kt = (dot(sl, qh, 0, 0) * scale).astype(BF)
        vt = dot(probl[h], gh, 0, 0).astype(BF)
        for a in range(NA):
            lg_p[a % NX, a // NX, h] = kt[a * LB : (a + 1) * LB]
            lg_p[a % NX, a // NX, HL + h] = vt[a * LB : (a + 1) * LB]
    lane1 = lax.broadcasted_iota(jnp.int32, (TB, 128), 1)
    sub1 = lax.broadcasted_iota(jnp.int32, (TB, 128), 0)
    innr[al] = jnp.sum(jnp.where(lane1 == sub1, inner, 0.0), axis=0, keepdims=True)
    qg_g.s1()
    in_g.s1()
    lg.s1()
    sum_line(1, 2, 3)
    qg_g.s2()
    in_g.s2()
    lg.s2()
    sum_line(1, 3, 4)

    ex_out.wait()
    branch = outp[ia].astype(F32)
    for k in range(1, NI):
        branch = branch + outr[k].astype(F32)
    up = up_ref[...].astype(F32)
    mixed_ref[...] = (st_ref[...].astype(F32) + gate * branch).astype(BF)
    gg_p[...] = jnp.sum(up * branch * (1.0 - gate * gate), axis=0, keepdims=True)
    ex_gi.start()

    qg_g.s3()
    in_g.s3()
    qg_rows = qgrow[...].reshape(TR, WD)
    grad_parts(states_rows, qg_rows, 0)
    sum_line(1, 4, 5)
    sum_line(0, 0, 1)
    times_rows_t(qg_rows, 0, normp)
    ex_norm.start()
    ex_in.start()
    lg.s3()
    sum_line(1, 5, 6)
    sum_line(0, 1, 2)
    ex_gi.wait()
    t = gg_p[...]
    for k in range(1, NI):
        t = t + gg_r[k]
    ggj[...] = t
    ex_gj.start()
    lg.s4()
    sum_line(1, 6, NJ)
    sum_line(0, 2, 3)
    lg.s5()
    gwo_ref[...] = sum_end(1).T.astype(F32)
    sum_line(0, 3, 4)
    lg.s6()
    ex_norm.wait()
    ex_in.wait()
    ng = normp[ia].astype(F32)
    inner = innr[ia]
    for k in range(1, NI):
        ng = ng + normr[k].astype(F32)
        inner = inner + rin[k]
    inner = jnp.sum(jnp.where(lane1 == sub1, inner, 0.0), axis=1, keepdims=True)
    gst_ref[...] = (up + ng - st_ref[...].astype(F32) * (inv_own * inner / D)).astype(BF)
    sum_line(0, 4, 5)
    lg.s7()
    total = jnp.zeros((NL, 128), F32)
    for h in range(HL):
        cols = slice(h * HS, (h + 1) * HS)
        kg = lg_full[:, h].reshape(NL, HS)
        vg = lg_full[:, HL + h].reshape(NL, HS)
        total = total + dot(kg, wk_ref[:, cols], 1, 1) + dot(vg, wv_ref[:, cols], 1, 1)
    rowi = lax.broadcasted_iota(jnp.int32, (NL, NL), 0)
    coli = lax.broadcasted_iota(jnp.int32, (NL, NL), 1)
    from_row = ((rowi // LR) % NJ) * LI + (rowi // (LR * NJ)) * LR + rowi % LR
    perm = (coli == from_row).astype(F32).astype(BF)
    gl[...] = dot(perm, total.astype(BF), 1, 0).astype(BF).reshape(NI, NJ * LR, 128)
    ex_gl.start()
    sum_line(0, 5, 6)
    for h in range(HL):
        cols = slice(h * HS, (h + 1) * HS)
        gwk_ref[:, cols] = dot(latt[...], lg_full[:, h].reshape(NL, HS), 1, 0)
        gwv_ref[:, cols] = dot(latt[...], lg_full[:, HL + h].reshape(NL, HS), 1, 0)
    ex_gl.wait()
    t = gl[ia].astype(F32)
    for k in range(1, NI):
        t = t + glr[k].astype(F32)
    wide_r = lax.broadcasted_iota(jnp.int32, (NJ * 16, NJ * LR), 0)
    wide_c = lax.broadcasted_iota(jnp.int32, (NJ * 16, NJ * LR), 1)
    wide = ((wide_r // 16 * LR + wide_r % 16 == wide_c) & (wide_r % 16 < LR)).astype(F32).astype(BF)
    gls[...] = dot(wide, t.astype(BF), 1, 0).astype(BF).reshape(NJ, 16, 128)
    glf[ja] = gls[ja]
    ex_g2.start()
    sum_line(0, 6, NJ)
    ex_gj.wait()
    t = ggj[...]
    for k in range(1, NJ):
        t = t + ggj_r[k]
    gg_ref[...] = t
    ex_g2.wait()
    for s in range(NJ):
        glat_ref[:, s * 128 : (s + 1) * 128] = glf[s, 0:LR, :]
    gwq_ref[...] = sum_end(0).astype(F32)
    for f in drains:
        f()


def run(sizes, *args):
    NI, NJ, NZ, NX = sizes
    st, lat, wq, wk, wv, wo, gate, img, cnt, up = args
    NA = NZ * NX
    TB, DL = st.shape
    WB, WD = wq.shape
    HL = WD // HS
    LR = lat.shape[0]
    LI = NI * LR
    NL = NJ * LI
    LB = NL // NA
    CB = 2 * HL
    TR = NI * TB
    assert CB == NJ and NI == NA and NZ <= 2 and DL == NJ * 128 and WB == 128
    vm = lambda dt, *s: pltpu.VMEM(s, dt)

    def allsum():
        return [
            vm(BF, NX, NZ, CB, LB, 128), vm(BF, NX, NZ, CB, LB, 128), vm(BF, NZ, CB, LB, 128), vm(BF, CB, LB, 128),
            vm(BF, CB, LB, 128), vm(BF, NJ, LB, 128), vm(BF, NA, CB, LB, 128),
        ]

    def scatter():
        return [
            vm(BF, NX, NZ, TB, WD), vm(BF, NX, NZ, TB, WD), vm(BF, NZ, TB, WD), vm(BF, TB, WD), vm(BF, TB, WD),
        ]

    scratch = [
        vm(BF, 2, NJ, CH, WB // CH, WD), vm(BF, NI, TB, DL), vm(BF, NI, TB, DL),
        vm(BF, NI, 16, DL), vm(BF, NJ, LI, 128), vm(BF, NJ, LI, 128), vm(BF, 128, NL),
        *allsum(), *allsum(), *scatter(), *scatter(),
        vm(F32, 1, TR), vm(F32, NX, 1, TR), vm(F32, 1, TR), vm(F32, 1, TR),
        vm(BF, NA, TB, WD), vm(BF, NA, TB, WD), vm(F32, NA, 1, 128), vm(F32, NI, 1, 128),
        vm(BF, NI, TB, DL), vm(BF, NI, TB, DL), vm(BF, NI, TB, DL), vm(BF, NI, TB, DL),
        vm(F32, 1, DL), vm(F32, NI, 1, DL), vm(F32, 1, DL), vm(F32, NJ, 1, DL),
        vm(BF, 2, NJ, WB, WD), vm(BF, 2, NJ, WB, WD), vm(BF, 2, NJ, WB, WD),
        vm(BF, NI, NJ * LR, 128), vm(BF, NI, NJ * LR, 128), vm(BF, NJ, 16, 128), vm(BF, NJ, 16, 128),
        vm(F32, HL, TB, NL), vm(BF, HL, TB, NL),
        pltpu.SemaphoreType.DMA((320,)), pltpu.SemaphoreType.DMA((320,)),
    ]
    v, s = pl.BlockSpec(memory_space=pltpu.VMEM), pl.BlockSpec(memory_space=pltpu.SMEM)
    shape = jax.ShapeDtypeStruct
    out = pl.pallas_call(
        functools.partial(kernel, sizes, DL),
        out_shape=(
            shape((TB, DL), BF), shape((TB, DL), BF), shape((LR, DL), BF), shape((WB, WD), F32),
            shape((WB, WD), F32), shape((WB, WD), F32), shape((WD, WB), F32), shape((1, DL), F32),
        ),
        in_specs=[v] * 8 + [s, v],
        out_specs=tuple([v] * 8),
        scratch_shapes=scratch,
        compiler_params=pltpu.CompilerParams(collective_id=0, has_side_effects=True, vmem_limit_bytes=56 * 2**20),
    )(st, lat, wq, wk, wv, wo, gate.reshape(1, DL), img.reshape(TB, 1), cnt, up)
    return (*out[:7], out[7].reshape(DL))


def solution(mesh, sizes=None):
    if sizes is None:
        sizes = (mesh.shape["ia"], mesh.shape["ja"], 2, mesh.shape["al"] // 2)
    tokens = P(("ja", "ia"), "al")
    weight = P(("al", "ja"), "ia")
    second = P("ia", ("al", "ja"))
    return jax.shard_map(
        functools.partial(run, sizes),
        mesh=mesh,
        in_specs=(tokens, tokens, weight, weight, weight, second, P("al"), P(("ja", "al")), P(), tokens),
        out_specs=(tokens, tokens, tokens, weight, weight, weight, second, P("al")),
        check_vma=False,
    )
```

time: 1610 us -> 196 us (0.12); the launches traced: 1580 us -> 196 us
  blocking collectives: 995 us -> 0 us
  waiting for transfers between devices: 529 us -> 0 us
  Pallas kernels: 0 us -> 186 us
  matrix products: 20.6 us -> 0 us
    psum x4 -> x0, blocking collectives: 741 us -> none  [the longest x1 465 us: body(): latent_grad = lax.psum(latent_term, ('ja', 'al')).astype(jnp.bfloat16)]
    all_gather x7 -> x0, blocking collectives: 255 us -> none  [the longest x1 57.4 us: body(): attended_rows = lax.all_gather(attended, 'al', axis=0, tiled=True)]
    reduce_scatter x5 -> x0, waiting for transfers between devices: 208 us -> none  [the longest x1 104 us: body(): lax.psum_scatter(query_part.astype(jnp.bfloat16), 'al', scatter_dimension...]
    pallas_call x0 -> x1, Pallas kernels: none -> 186 us  [run(): pl.pallas_call(functools.partial(kernel, sizes, DL), out_shape=(shape((TB...]
    psum x1 -> x0, waiting for transfers between devices: 145 us -> none  [body(): kv_total = lax.psum(kv_part.astype(jnp.bfloat16), 'al')]
    all_gather x4 -> x0, waiting for transfers between devices: 139 us -> none  [the longest x1 55 us: body(): lax.all_gather(w_output, 'ja', axis=1, tiled=True)]
    unnamed x14 -> x0, waiting for transfers between devices: 36.6 us -> none
    dot_general x17 -> x0, matrix products: 19.5 us -> none  [the longest x4 7.35 us: contract_last(): lax.dot_general(left_side, right_side, (((1,), (1,)), ((), ())), preferre...]
  transfers between devices with their start and end apart: 12 -> 0, of which waited for: 8 -> 0; matrix products, arithmetic and copies ran while one was open for 2% -> 0% of each run, Pallas kernels for 0% -> 0%
where the time goes in v1:
time: 196 us
  Pallas kernels  186 us (95%)
  local copies, waits for them, and re-layouts  9.38 us (5%)
    pallas_call x1, Pallas kernels, run(): pl.pallas_call(functools.partial(kernel, sizes, DL), out_shape=(shape((TB...  186 us
    unnamed x22, local copies, waits for them, and re-layouts  8.68 us

profile of v1, /device:TPU:1, one launch (start us, length us, event | category | flops | bytes accessed | tf_op | source)
XLA Modules:
  0.0 196.0 jit_solution(4194505270619004707)
XLA Ops:
  0.6 0.0 copy-start.6
  0.6 0.6 copy-done.6
  1.3 0.7 copy.18.refs_7_
  2.0 185.9 %shard_map.161 = (bf16[32,1024]{1,0:T(8,128)(2,1)}, bf16[32,1024]{1,0:T(8,128)(2,1)}, bf16[4,1024]{1,0:T(4,128)(2,1)}, f32[128,512]{1,0:T(8,128)}, f32[128,512]{...) custom-call(bf16[32,1024]{1,0:T(8,128)(2,1)} %refs_0_.1, bf16[4,1024]{1,0:T(4,128)(2,1)} %refs_1_.1, ...), custom_call_target="tpu_custom_call" | custom-call | tf_op jit(solution)/shard_map/pallas_call | solution.py:638
  187.9 0.0 copy-start.3
  187.9 1.5 copy.27
  189.4 0.0 copy-start.4
  189.4 1.5 copy.28
  190.9 0.0 copy-done.4
  190.9 0.6 copy.29
  191.5 0.0 copy-done.3
  191.5 0.0 copy-start.2
  191.5 0.7 copy.30
  192.2 0.3 copy-done.2
  192.6 0.0 copy-start.1
  192.6 0.7 copy.31
  193.3 0.3 copy-done.1
  193.6 0.0 copy-start
  193.6 0.7 copy.32
  194.3 0.3 copy-done
  194.7 0.0 copy-start.5
  194.7 0.7 copy.33
  195.4 0.0 copy-done.5
  195.4 0.6 copy.34
Async XLA Ops:
  0.6 0.7 copy-start.6
  187.9 3.6 %copy-start.3 = (f32[128,512]{1,0:T(8,128)S(1)}, f32[128,512]{1,0:T(8,128)}, u32[]{:S(2)}) copy-start(f32[128,512]{1,0:T(8,128)} %get-tuple-element.35) | copy-start | bytes 786436
  189.4 1.5 copy-start.4
  191.5 1.0 copy-start.2
  192.6 1.0 copy-start.1
  193.6 1.0 copy-start
  194.7 0.7 copy-start.5

commit v2 on v1

v2 whole, which is shorter than its diff:
```python
import functools
import math

import jax
import jax.numpy as jnp
from jax import lax
from jax.experimental import pallas as pl
from jax.experimental.pallas import tpu as pltpu
from jax.sharding import PartitionSpec as P

MESH = pl.DeviceIdType.MESH
D = 8192
EPS = 1e-05
BF = jnp.bfloat16
F32 = jnp.float32
IMGS = 4
HS = 128


def dot(a, b, ca, cb):
    return lax.dot_general(a, b, (((ca,), (cb,)), ((), ())), preferred_element_type=F32)


def loop(lo, hi, f):
    lax.fori_loop(lo, hi, lambda i, c: (f(i), c)[1], 0)


def kernel(sizes, *refs):
    NI, NJ, NZ, NX = sizes
    (
        st_ref, lat_ref, wq_ref, wk_ref, wv_ref, wo_ref, gate_ref, img_ref, cnt_ref, up_ref,
        mixed_ref, gst_ref, glat_ref, gwq_ref, gwk_ref, gwv_ref, gwo_ref, gg_ref,
    ) = refs[:18]
    (
        W, latg, latc, latb, latt,
        s0, s1, s2, s3, strow,
        b0, b1, b2, b3, brrow,
        kv_p, kv_rx, kv_zs, kv_rz, kv_full,
        lg_p, lg_rx, lg_zs, lg_rz, lg_full,
        q_p, q_rr, q_rl, qs,
        a_p, a_rr, a_rl, gs,
        e_p, e_r, im_z, im_x,
        atrow, qgrow, innr, rin,
        outp, outr, out1, out2, out3,
        normp, normr, norm1, norm2, norm3,
        gg_p, gg_r, ggj, ggj_r,
        gp, gpr,
        gl, glr, gls, glf,
        prob, probl,
        ssem, rsem,
    ) = refs[18:]
    NA, NR = NZ * NX, NZ * NJ
    TB, DL = st_ref.shape
    WB, WD = wq_ref.shape
    HL = WD // HS
    LR = lat_ref.shape[0]
    LI = NI * LR
    NL = NJ * LI
    LB = NL // NA
    LAT = NL // IMGS
    CB = 2 * HL
    TG = NR * TB
    DG = NX * WB
    scale = 1.0 / math.sqrt(HS)

    ia, ja, al = lax.axis_index("ia"), lax.axis_index("ja"), lax.axis_index("al")
    x, zh = al % NX, al // NX
    z = zh * NJ + ja
    place = {"ia": (ia, NI), "ja": (ja, NJ), "x": (x, NX), "z": (z, NR)}

    def device(axis, i):
        if axis == "x":
            return {"al": zh * NX + i}
        if axis == "z":
            return {"ja": i % NJ, "al": (i // NJ) * NX + x}
        return {axis: i}

    used = [0]
    drains = []

    def take(n):
        used[0] += n
        assert used[0] <= ssem.shape[0]
        return used[0] - n

    def copy(src, dst, i, dev):
        return pltpu.make_async_remote_copy(
            src_ref=src, dst_ref=dst, send_sem=ssem.at[i], recv_sem=rsem.at[i],
            device_id=dev, device_id_type=MESH,
        )

    class Exchange:
        def __init__(self, axis, src, dst):
            self.axis, self.src, self.dst = axis, src, dst
            self.me, self.n = place[axis]
            self.base = take(self.n)

        def out(self, k):
            peer = (self.me + k) % self.n
            return copy(self.src(peer), self.dst(self.me, k), self.base + k, device(self.axis, peer))

        def into(self, k):
            peer = (self.me - k + self.n) % self.n
            return copy(self.src(peer), self.dst(peer, k), self.base + k, device(self.axis, peer))

        def start(self):
            loop(1, self.n, lambda k: self.out(k).start())
            drains.append(lambda: loop(1, self.n, lambda k: self.out(k).wait_send()))

        def wait(self):
            loop(1, self.n, lambda k: self.into(k).wait_recv())

    FAR, NEAR = NR // 2, NR - 1 - NR // 2
    right, left = device("z", (z + 1) % NR), device("z", (z + NR - 1) % NR)

    class RingSum:
        def __init__(self, p, rr, rl):
            self.p, self.rr, self.rl = p, rr, rl
            self.r, self.l = take(FAR), take(NEAR)

        def go_right(self, s, src):
            return copy(src, self.rr.at[s], self.r + s, right)

        def go_left(self, s, src):
            return copy(src, self.rl.at[s], self.l + s, left)

        def step(self, s):
            p, rr, rl = self.p, self.rr, self.rl
            if s == 0:
                self.go_right(0, p.at[(z + FAR) % NR]).start()
                self.go_left(0, p.at[(z + NR - NEAR) % NR]).start()
                return
            if s < FAR:
                self.go_right(s - 1, rr.at[s - 1]).wait_recv()
                rr[s - 1] = (rr[s - 1].astype(F32) + p[(z + FAR - s) % NR].astype(F32)).astype(BF)
                self.go_right(s, rr.at[s - 1]).start()
            if s < NEAR:
                self.go_left(s - 1, rl.at[s - 1]).wait_recv()
                rl[s - 1] = (rl[s - 1].astype(F32) + p[(z + NR - NEAR + s) % NR].astype(F32)).astype(BF)
                self.go_left(s, rl.at[s - 1]).start()

        def end(self):
            self.go_right(FAR - 1, self.rr.at[FAR - 1]).wait_recv()
            self.go_left(NEAR - 1, self.rl.at[NEAR - 1]).wait_recv()

            def drain():
                for s in range(FAR):
                    self.go_right(s, self.rr.at[s]).wait_send()
                for s in range(NEAR):
                    self.go_left(s, self.rl.at[s]).wait_send()

            drains.append(drain)
            return self.p[z].astype(F32) + self.rr[FAR - 1].astype(F32) + self.rl[NEAR - 1].astype(F32)

    class RingGather:
        def __init__(self, buf):
            self.buf = buf
            self.r, self.l = take(FAR), take(NEAR)

        def go_right(self, s):
            b = self.buf.at[(z - s + NR) % NR]
            return copy(b, b, self.r + s, right)

        def go_left(self, s):
            b = self.buf.at[(z + s) % NR]
            return copy(b, b, self.l + s, left)

        def step(self, s):
            if s < FAR:
                if s > 0:
                    self.go_right(s - 1).wait_recv()
                self.go_right(s).start()
            if s < NEAR:
                if s > 0:
                    self.go_left(s - 1).wait_recv()
                self.go_left(s).start()

        def end(self):
            self.go_right(FAR - 1).wait_recv()
            self.go_left(NEAR - 1).wait_recv()

            def drain():
                for s in range(FAR):
                    self.go_right(s).wait_send()
                for s in range(NEAR):
                    self.go_left(s).wait_send()

            drains.append(drain)

    class AllSum:
        def __init__(self, p, rx, zs, rz, full):
            self.p, self.rx, self.zs, self.rz, self.full = p, rx, zs, rz, full
            self.x1 = Exchange("x", lambda peer: p.at[peer], lambda s, k: rx.at[k])
            self.z1 = Exchange("z", lambda peer: zs.at[peer // NJ, peer % NJ], lambda s, k: rz.at[k])
            self.z2 = Exchange("z", lambda peer: full.at[x, zh, ja], lambda s, k: full.at[x, s // NJ, s % NJ])
            self.x2 = Exchange("x", lambda peer: full.at[x], lambda s, k: full.at[s])

        def a(self):
            self.x1.start()

        def b(self):
            self.x1.wait()
            t = self.p[x].astype(F32)
            for k in range(1, NX):
                t = t + self.rx[k].astype(F32)
            self.zs[...] = t.astype(BF)
            self.z1.start()

        def c(self):
            self.z1.wait()
            t = self.zs[zh, ja].astype(F32)
            for k in range(1, NR):
                t = t + self.rz[k].astype(F32)
            self.full[x, zh, ja] = t.astype(BF)
            self.z2.start()

        def d(self):
            self.z2.wait()
            self.x2.start()

        def e(self):
            self.x2.wait()

        def head(self, h):
            return jnp.concatenate([self.full[a % NX, a // NX, h] for a in range(NA)], axis=0)

    class Spread:
        def __init__(self, t0, t1, t2, t3, rows):
            self.t0, self.t1, self.t2, self.t3, self.rows = t0, t1, t2, t3, rows
            self.z = Exchange("ja", lambda peer: t0.at[peer], lambda s, k: t1.at[s // NZ, s % NZ])
            self.x = Exchange("x", lambda peer: t1.at[peer], lambda s, k: t2.at[s])
            self.y = Exchange("ia", lambda peer: t3.at[ia], lambda s, k: t3.at[s])

        def load(self, v):
            for s in range(NJ):
                self.t0[s] = v[:, s * WB : (s + 1) * WB]
            self.t1[ja // NZ, ja % NZ] = self.t0[ja]

        def a(self):
            self.z.start()

        def b(self):
            self.z.wait()
            self.x.start()

        def c(self):
            self.x.wait()
            self.t2[x] = self.t1[x]
            self.t3[ia] = self.t2[...]
            self.y.start()

        def d(self):
            self.y.wait()
            for k in range(NX):
                for j in range(NZ):
                    self.rows[j * NI * TB : (j + 1) * NI * TB, k * WB : (k + 1) * WB] = self.t3[:, k, j].reshape(NI * TB, WB)

    class Collect:
        def __init__(self, p, r, t1, t2, t3):
            self.p, self.r, self.t1, self.t2, self.t3 = p, r, t1, t2, t3
            self.y = Exchange("ia", lambda peer: p.at[peer], lambda s, k: r.at[k])
            self.x = Exchange("x", lambda peer: t1.at[peer], lambda s, k: t2.at[s])
            self.z = Exchange("ja", lambda peer: t2.at[peer // NZ, peer % NZ], lambda s, k: t3.at[s])

        def a(self, rows, m):
            for k in range(NX):
                v = dot(rows, W[m, k], 1, 1).astype(BF)
                for j in range(NZ):
                    self.p[:, k, j] = v[j * NI * TB : (j + 1) * NI * TB].reshape(NI, TB, WB)
            self.y.start()

        def b(self, correct=None):
            self.y.wait()
            t = self.p[ia].astype(F32)
            for k in range(1, NI):
                t = t + self.r[k].astype(F32)
            if correct is not None:
                t = correct(t)
            self.t1[...] = t.astype(BF)
            self.t2[x] = self.t1[x]
            self.x.start()

        def c(self):
            self.x.wait()
            self.t3[ja] = self.t2[ja // NZ, ja % NZ]
            self.z.start()

        def d(self):
            self.z.wait()
            return jnp.concatenate([self.t3[s] for s in range(NJ)], axis=1).astype(F32)

    ex_wq = Exchange("x", lambda peer: W.at[0, x], lambda s, k: W.at[0, s])
    ex_wo = Exchange("x", lambda peer: W.at[1, x], lambda s, k: W.at[1, s])
    ex_lat = Exchange("ia", lambda peer: latg.at[ia], lambda s, k: latg.at[s])
    ex_l2 = Exchange("ja", lambda peer: latc.at[peer], lambda s, k: latb.at[s])
    sp_s, sp_b = Spread(s0, s1, s2, s3, strow), Spread(b0, b1, b2, b3, brrow)
    kv = AllSum(kv_p, kv_rx, kv_zs, kv_rz, kv_full)
    lg = AllSum(lg_p, lg_rx, lg_zs, lg_rz, lg_full)
    q_s, a_s = RingSum(q_p, q_rr, q_rl), RingSum(a_p, a_rr, a_rl)
    e_z = Exchange("z", lambda peer: e_p, lambda s, k: e_r.at[k])
    ex_iz = Exchange("z", lambda peer: im_z.at[z], lambda s, k: im_z.at[s])
    ex_ix = Exchange("x", lambda peer: im_x.at[x], lambda s, k: im_x.at[s])
    at_g, qg_g = RingGather(atrow), RingGather(qgrow)
    in_g = Exchange("z", lambda peer: innr.at[ja, zh], lambda s, k: innr.at[s % NJ, s // NJ])
    ex_in = Exchange("ia", lambda peer: innr.at[peer], lambda s, k: rin.at[k])
    c_out, c_norm = Collect(outp, outr, out1, out2, out3), Collect(normp, normr, norm1, norm2, norm3)
    ex_gi = Exchange("ia", lambda peer: gg_p, lambda s, k: gg_r.at[k])
    ex_gj = Exchange("ja", lambda peer: ggj, lambda s, k: ggj_r.at[k])
    ex_gq = Exchange("x", lambda peer: gp.at[0, peer], lambda s, k: gpr.at[0, k])
    ex_go = Exchange("x", lambda peer: gp.at[1, peer], lambda s, k: gpr.at[1, k])
    ex_gl = Exchange("ia", lambda peer: gl.at[peer], lambda s, k: glr.at[k])
    ex_g2 = Exchange("ja", lambda peer: gls.at[peer], lambda s, k: glf.at[s])

    barrier = pltpu.get_barrier_semaphore()
    for axis in ("ia", "x", "z"):
        i, n = place[axis]
        loop(1, n, lambda k: pl.semaphore_signal(barrier, 1, device_id=device(axis, (i + k) % n), device_id_type=MESH))

    lane1 = lax.broadcasted_iota(jnp.int32, (TB, 128), 1)
    sub1 = lax.broadcasted_iota(jnp.int32, (TB, 128), 0)

    def to_row(col):
        return jnp.sum(jnp.where(lane1 == sub1, col, 0.0), axis=0, keepdims=True)

    def to_col(row):
        return jnp.sum(jnp.where(lane1 == sub1, row, 0.0), axis=1, keepdims=True)

    sp_s.load(st_ref[...])
    latg[ia] = jnp.zeros((16, DL), BF)
    latg[ia, 0:LR, :] = lat_ref[...]
    W[0, x] = wq_ref[...]
    gate = jnp.tanh(gate_ref[...])
    sp_b.load((up_ref[...].astype(F32) * gate).astype(BF))
    im_z[z] = to_row(img_ref[...].astype(F32))
    pl.semaphore_wait(barrier, NI - 1 + NX - 1 + NR - 1)

    sp_s.a()
    ex_lat.start()
    sp_b.a()
    ex_wq.start()
    ex_iz.start()
    W[1, x] = wo_ref[...].T
    ex_wo.start()

    sp_s.b()
    ex_lat.wait()
    pick_r = lax.broadcasted_iota(jnp.int32, (LI, NI * 16), 0)
    pick_c = lax.broadcasted_iota(jnp.int32, (LI, NI * 16), 1)
    pick = (pick_c == (pick_r // LR) * 16 + pick_r % LR).astype(F32).astype(BF)
    packed = dot(pick, latg[...].reshape(NI * 16, DL), 1, 0).astype(BF)
    for s in range(NJ):
        latc[s] = packed[:, s * 128 : (s + 1) * 128]
    latb[ja] = latc[ja]
    ex_l2.start()
    sp_b.b()
    sp_s.c()
    sp_b.c()

    ex_l2.wait()
    lat = latb[...].reshape(NL, 128)
    latt[...] = lat.T
    for h in range(CB):
        wref = wk_ref if h < HL else wv_ref
        c = h % HL
        part = dot(lat, wref[:, c * HS : (c + 1) * HS], 1, 0).astype(BF)
        for a in range(NA):
            kv_p[a % NX, a // NX, h] = part[a * LB : (a + 1) * LB]
    kv.a()
    ex_iz.wait()
    im_x[x] = im_z[...]
    ex_ix.start()

    def rows_times(rows, m, p):
        acc = dot(rows, W[m].reshape(DG, WD), 1, 0).astype(BF)
        for d in range(NR):
            p[d] = acc[d * TB : (d + 1) * TB]

    sp_s.d()
    ex_wq.wait()
    rows_times(strow[...], 0, q_p)
    q_s.step(0)
    kv.b()
    sq = strow[...].astype(F32)
    sq = (sq * sq).astype(BF)
    e_p[...] = dot(jnp.ones((8, DG), BF), sq, 1, 1)[0:1]
    e_z.start()
    q_s.step(1)
    sp_b.d()
    ex_wo.wait()
    rows_times(brrow[...], 1, a_p)
    q_s.step(2)
    a_s.step(0)
    kv.c()
    q_s.step(3)
    a_s.step(1)
    q_s.step(4)
    a_s.step(2)
    kv.d()
    q_s.step(5)
    a_s.step(3)
    e_z.wait()
    energy = e_p[...]
    for k in range(1, NR):
        energy = energy + e_r[k]
    inv_row = lax.rsqrt(energy / D + EPS)
    lane = lax.broadcasted_iota(jnp.int32, (TB, TG), 1)
    sub = lax.broadcasted_iota(jnp.int32, (TB, TG), 0)

    def column(block):
        return jnp.sum(jnp.where(lane == block * TB + sub, inv_row, 0.0), axis=1, keepdims=True)

    inv_attn = column(z)
    ex_ix.wait()
    image_col = to_col(im_x[ja % NX, (ja // NX) * NJ + NZ * x + zh])
    slot = lax.broadcasted_iota(jnp.int32, (TB, NL), 1)
    image = slot // LAT
    count = jnp.where(image == 0, cnt_ref[0], jnp.where(image == 1, cnt_ref[1], jnp.where(image == 2, cnt_ref[2], cnt_ref[3])))
    allowed = (image_col == image.astype(F32)) & (slot % LAT < count)
    for s in range(6, FAR):
        q_s.step(s)
        a_s.step(s - 2)
    kv.e()
    q = q_s.end() * inv_attn
    qs[...] = q.astype(BF)
    for h in range(HL):
        cols = slice(h * HS, (h + 1) * HS)
        sco = dot(qs[:, cols], kv.head(h), 1, 1) * scale
        raised = jnp.where(allowed, jnp.exp(sco), 0.0)
        pr = raised / jnp.sum(raised, axis=1, keepdims=True)
        prob[h] = pr
        probl[h] = pr.astype(BF)
        atrow[z, :, cols] = dot(probl[h], kv.head(HL + h), 1, 0).astype(BF)
    at_g.step(0)
    for s in range(max(FAR - 2, 4), FAR):
        a_s.step(s)
    at_g.step(1)

    gs[...] = a_s.end().astype(BF)
    at_g.step(2)
    inner = jnp.zeros((TB, 1), F32)
    for h in range(HL):
        cols = slice(h * HS, (h + 1) * HS)
        kh = kv.head(h)
        gh = gs[:, cols]
        qh = qs[:, cols]
        pg = dot(gh, kv.head(HL + h), 1, 1)
        pr = prob[h]
        sg = pr * (pg - jnp.sum(pr * pg, axis=1, keepdims=True))
        sl = sg.astype(BF)
        qg = dot(sl, kh, 1, 0) * scale * inv_attn
        inner = inner + jnp.sum(qg * qh.astype(F32), axis=1, keepdims=True)
        qgrow[z, :, cols] = qg.astype(BF)
        kt = (dot(sl, qh, 0, 0) * scale).astype(BF)
        vt = dot(probl[h], gh, 0, 0).astype(BF)
        for a in range(NA):
            lg_p[a % NX, a // NX, h] = kt[a * LB : (a + 1) * LB]
            lg_p[a % NX, a // NX, HL + h] = vt[a * LB : (a + 1) * LB]
    qg_g.step(0)
    innr[ja, zh] = to_row(inner)
    in_g.start()
    lg.a()
    at_g.step(3)
    qg_g.step(1)
    at_g.step(4)
    qg_g.step(2)
    lg.b()
    for s in range(5, FAR):
        at_g.step(s)
        qg_g.step(s - 2)
    at_g.end()

    def grad_parts(left_rows, right_rows, m):
        for k in range(NX):
            gp[m, k] = dot(left_rows[:, k * WB : (k + 1) * WB], right_rows, 0, 0).astype(BF)

    def grad_sum(m):
        t = gp[m, x].astype(F32)
        for k in range(1, NX):
            t = t + gpr[m, k].astype(F32)
        return t

    attn_rows = atrow[...].reshape(TG, WD)
    c_out.a(attn_rows, 1)
    for s in range(max(FAR - 2, 3), FAR):
        qg_g.step(s)
    lg.c()
    grad_parts(brrow[...], attn_rows, 1)
    ex_go.start()
    in_g.wait()
    ex_in.start()
    qg_g.end()
    qg_rows = qgrow[...].reshape(TG, WD)
    c_norm.a(qg_rows, 0)
    c_out.b()
    grad_parts(strow[...], qg_rows, 0)
    ex_gq.start()
    lg.d()
    c_out.c()

    def correct(t):
        ex_in.wait()
        own = innr[ia]
        for k in range(1, NI):
            own = own + rin[k]
        parts = []
        for j in range(NZ):
            coef = column(j * NI + ia) * to_col(own[j]) / D
            parts.append(t[:, j] - s2[:, j].astype(F32) * coef[None])
        return jnp.stack(parts, axis=1)

    c_norm.b(correct)
    up = up_ref[...].astype(F32)
    branch = c_out.d()
    mixed_ref[...] = (st_ref[...].astype(F32) + gate * branch).astype(BF)
    gg_p[...] = jnp.sum(up * branch * (1.0 - gate * gate), axis=0, keepdims=True)
    ex_gi.start()
    c_norm.c()
    lg.e()
    total = jnp.zeros((NL, 128), F32)
    for h in range(HL):
        cols = slice(h * HS, (h + 1) * HS)
        total = total + dot(lg.head(h), wk_ref[:, cols], 1, 1) + dot(lg.head(HL + h), wv_ref[:, cols], 1, 1)
    rowi = lax.broadcasted_iota(jnp.int32, (NL, NL), 0)
    coli = lax.broadcasted_iota(jnp.int32, (NL, NL), 1)
    from_row = ((rowi // LR) % NJ) * LI + (rowi // (LR * NJ)) * LR + rowi % LR
    perm = (coli == from_row).astype(F32).astype(BF)
    gl[...] = dot(perm, total.astype(BF), 1, 0).astype(BF).reshape(NI, NJ * LR, 128)
    ex_gl.start()
    ex_gi.wait()
    t = gg_p[...]
    for k in range(1, NI):
        t = t + gg_r[k]
    ggj[...] = t
    ex_gj.start()
    for h in range(HL):
        cols = slice(h * HS, (h + 1) * HS)
        gwk_ref[:, cols] = dot(latt[...], lg.head(h), 1, 0)
        gwv_ref[:, cols] = dot(latt[...], lg.head(HL + h), 1, 0)
    ex_gl.wait()
    t = gl[ia].astype(F32)
    for k in range(1, NI):
        t = t + glr[k].astype(F32)
    wide_r = lax.broadcasted_iota(jnp.int32, (NJ * 16, NJ * LR), 0)
    wide_c = lax.broadcasted_iota(jnp.int32, (NJ * 16, NJ * LR), 1)
    wide = ((wide_r // 16 * LR + wide_r % 16 == wide_c) & (wide_r % 16 < LR)).astype(F32).astype(BF)
    gls[...] = dot(wide, t.astype(BF), 1, 0).astype(BF).reshape(NJ, 16, 128)
    glf[ja] = gls[ja]
    ex_g2.start()
    gst_ref[...] = (up + c_norm.d()).astype(BF)
    ex_go.wait()
    gwo_ref[...] = grad_sum(1).T
    ex_gq.wait()
    gwq_ref[...] = grad_sum(0)
    ex_gj.wait()
    t = ggj[...]
    for k in range(1, NJ):
        t = t + ggj_r[k]
    gg_ref[...] = t
    ex_g2.wait()
    for s in range(NJ):
        glat_ref[:, s * 128 : (s + 1) * 128] = glf[s, 0:LR, :]
    for f in drains:
        f()


def run(sizes, *args):
    NI, NJ, NZ, NX = sizes
    st, lat, wq, wk, wv, wo, gate, img, cnt, up = args
    NA, NR = NZ * NX, NZ * NJ
    TB, DL = st.shape
    WB, WD = wq.shape
    HL = WD // HS
    LR = lat.shape[0]
    LI = NI * LR
    NL = NJ * LI
    LB = NL // NA
    CB = 2 * HL
    TG, DG = NR * TB, NX * WB
    assert CB == NJ and NI == NJ and NZ == 2 and NJ == NZ * NX and DL == NJ * 128 and WB == 128 and TB <= 128
    vm = lambda dt, *s: pltpu.VMEM(s, dt)

    def spread():
        return [
            vm(BF, NJ, TB, WB), vm(BF, NX, NZ, TB, WB), vm(BF, NX, NZ, TB, WB), vm(BF, NI, NX, NZ, TB, WB), vm(BF, TG, DG),
        ]

    def allsum():
        return [
            vm(BF, NX, NZ, CB, LB, 128), vm(BF, NX, NZ, CB, LB, 128), vm(BF, NZ, CB, LB, 128), vm(BF, NR, LB, 128),
            vm(BF, NX, NZ, CB, LB, 128),
        ]

    def ringsum():
        return [vm(BF, NR, TB, WD), vm(BF, NR // 2, TB, WD), vm(BF, NR - 1 - NR // 2, TB, WD), vm(BF, TB, WD)]

    def collect():
        return [
            vm(BF, NI, NX, NZ, TB, WB), vm(BF, NI, NX, NZ, TB, WB), vm(BF, NX, NZ, TB, WB), vm(BF, NX, NZ, TB, WB),
            vm(BF, NJ, TB, WB),
        ]

    scratch = [
        vm(BF, 2, NX, WB, WD), vm(BF, NI, 16, DL), vm(BF, NJ, LI, 128), vm(BF, NJ, LI, 128), vm(BF, 128, NL),
        *spread(), *spread(), *allsum(), *allsum(), *ringsum(), *ringsum(),
        vm(F32, 1, TG), vm(F32, NR, 1, TG), vm(F32, NR, 1, 128), vm(F32, NX, NR, 1, 128),
        vm(BF, NR, TB, WD), vm(BF, NR, TB, WD), vm(F32, NJ, NZ, 1, 128), vm(F32, NI, NZ, 1, 128),
        *collect(), *collect(),
        vm(F32, 1, DL), vm(F32, NI, 1, DL), vm(F32, 1, DL), vm(F32, NJ, 1, DL),
        vm(BF, 2, NX, WB, WD), vm(BF, 2, NX, WB, WD),
        vm(BF, NI, NJ * LR, 128), vm(BF, NI, NJ * LR, 128), vm(BF, NJ, 16, 128), vm(BF, NJ, 16, 128),
        vm(F32, HL, TB, NL), vm(BF, HL, TB, NL),
        pltpu.SemaphoreType.DMA((420,)), pltpu.SemaphoreType.DMA((420,)),
    ]
    v, s = pl.BlockSpec(memory_space=pltpu.VMEM), pl.BlockSpec(memory_space=pltpu.SMEM)
    shape = jax.ShapeDtypeStruct
    out = pl.pallas_call(
        functools.partial(kernel, sizes),
        out_shape=(
            shape((TB, DL), BF), shape((TB, DL), BF), shape((LR, DL), BF), shape((WB, WD), F32),
            shape((WB, WD), F32), shape((WB, WD), F32), shape((WD, WB), F32), shape((1, DL), F32),
        ),
        in_specs=[v] * 8 + [s, v],
        out_specs=tuple([v] * 8),
        scratch_shapes=scratch,
        compiler_params=pltpu.CompilerParams(collective_id=0, has_side_effects=True, vmem_limit_bytes=56 * 2**20),
    )(st, lat, wq, wk, wv, wo, gate.reshape(1, DL), img.reshape(TB, 1), cnt, up)
    return (*out[:7], out[7].reshape(DL))


def solution(mesh, sizes=None):
    if sizes is None:
        sizes = (mesh.shape["ia"], mesh.shape["ja"], 2, mesh.shape["al"] // 2)
    tokens = P(("ja", "ia"), "al")
    weight = P(("al", "ja"), "ia")
    second = P("ia", ("al", "ja"))
    return jax.shard_map(
        functools.partial(run, sizes),
        mesh=mesh,
        in_specs=(tokens, tokens, weight, weight, weight, second, P("al"), P(("ja", "al")), P(), tokens),
        out_specs=(tokens, tokens, tokens, weight, weight, weight, second, P("al")),
        check_vma=False,
    )
```

time: 196 us -> 161 us (0.82)
  Pallas kernels: 186 us -> 151 us
    pallas_call x1, Pallas kernels: 186 us -> 151 us  [run(): pl.pallas_call(functools.partial(kernel, sizes), out_shape=(shape((TB, DL...]
where the time goes in v2:
time: 161 us
  Pallas kernels  151 us (94%)
  local copies, waits for them, and re-layouts  9.38 us (6%)
    pallas_call x1, Pallas kernels, run(): pl.pallas_call(functools.partial(kernel, sizes), out_shape=(shape((TB, DL...  151 us
    unnamed x22, local copies, waits for them, and re-layouts  8.68 us

profile of v2, /device:TPU:1, one launch (start us, length us, event | category | flops | bytes accessed | tf_op | source)
XLA Modules:
  0.0 160.6 jit_solution(12149993073938090190)
XLA Ops:
  0.6 0.0 copy-start.6
  0.6 0.6 copy-done.6
  1.3 0.7 copy.18.refs_7_
  2.0 150.5 %shard_map.161 = (bf16[32,1024]{1,0:T(8,128)(2,1)}, bf16[32,1024]{1,0:T(8,128)(2,1)}, bf16[4,1024]{1,0:T(4,128)(2,1)}, f32[128,512]{1,0:T(8,128)}, f32[128,512]{...) custom-call(bf16[32,1024]{1,0:T(8,128)(2,1)} %refs_0_.1, bf16[4,1024]{1,0:T(4,128)(2,1)} %refs_1_.1, ...), custom_call_target="tpu_custom_call" | custom-call | tf_op jit(solution)/shard_map/pallas_call | solution.py:616
  152.5 0.0 copy-start.3
  152.5 1.5 copy.27
  154.0 0.0 copy-start.4
  154.1 1.5 copy.28
  155.5 0.0 copy-done.4
  155.5 0.6 copy.29
  156.1 0.0 copy-done.3
  156.1 0.0 copy-start.2
  156.1 0.7 copy.30
  156.8 0.3 copy-done.2
  157.2 0.0 copy-start.1
  157.2 0.7 copy.31
  157.9 0.3 copy-done.1
  158.2 0.0 copy-start
  158.2 0.7 copy.32
  158.9 0.3 copy-done
  159.3 0.0 copy-start.5
  159.3 0.7 copy.33
  160.0 0.0 copy-done.5
  160.0 0.6 copy.34
Async XLA Ops:
  0.6 0.7 copy-start.6
  152.5 3.6 %copy-start.3 = (f32[128,512]{1,0:T(8,128)S(1)}, f32[128,512]{1,0:T(8,128)}, u32[]{:S(2)}) copy-start(f32[128,512]{1,0:T(8,128)} %get-tuple-element.35) | copy-start | bytes 786436
  154.0 1.5 copy-start.4
  156.1 1.0 copy-start.2
  157.2 1.0 copy-start.1
  158.2 1.0 copy-start
  159.3 0.7 copy-start.5

commit v3 on v2

--- a/solution.py
+++ b/solution.py
@@ -110,80 +110,99 @@
         def wait(self):
             loop(1, self.n, lambda k: self.into(k).wait_recv())
 
-    FAR, NEAR = NR // 2, NR - 1 - NR // 2
-    right, left = device("z", (z + 1) % NR), device("z", (z + NR - 1) % NR)
+    HOPS = NR // 4
+    ring = {d: device("z", (z + d + NR) % NR) for d in (-2, -1, 1, 2)}
 
     class RingSum:
-        def __init__(self, p, rr, rl):
-            self.p, self.rr, self.rl = p, rr, rl
-            self.r, self.l = take(FAR), take(NEAR)
-
-        def go_right(self, s, src):
-            return copy(src, self.rr.at[s], self.r + s, right)
-
-        def go_left(self, s, src):
-            return copy(src, self.rl.at[s], self.l + s, left)
+        def __init__(self, p, odd, even):
+            self.p, self.odd, self.even = p, odd, even
+            self.o = {g: take(HOPS) for g in (1, -1)}
+            self.e = {g: take(HOPS) for g in (1, -1)}
+
+        def block(self, g, off):
+            return self.p.at[(z + g * off + NR) % NR]
+
+        def one(self, g, i, src=None):
+            dst = self.odd.at[(1 - g) // 2, i]
+            return copy(dst if src is None else src, dst, self.o[g] + i, ring[g])
+
+        def two(self, g, s, src=None):
+            dst = self.even.at[(1 - g) // 2, s]
+            return copy(dst if src is None else src, dst, self.e[g] + s, ring[2 * g])
+
+        def source(self, g, s):
+            if s == 0:
+                return self.block(1, 2 * HOPS)
+            return self.odd.at[1, 0] if g < 0 and s == 1 else self.even.at[(1 - g) // 2, s - 1]
 
         def step(self, s):
-            p, rr, rl = self.p, self.rr, self.rl
             if s == 0:
-                self.go_right(0, p.at[(z + FAR) % NR]).start()
-                self.go_left(0, p.at[(z + NR - NEAR) % NR]).start()
+                self.two(1, 0, self.source(1, 0)).start()
+                for i in range(HOPS):
+                    for g in (1, -1):
+                        self.one(g, i, self.block(g, 2 * HOPS - 1 - 2 * i)).start()
                 return
-            if s < FAR:
-                self.go_right(s - 1, rr.at[s - 1]).wait_recv()
-                rr[s - 1] = (rr[s - 1].astype(F32) + p[(z + FAR - s) % NR].astype(F32)).astype(BF)
-                self.go_right(s, rr.at[s - 1]).start()
-            if s < NEAR:
-                self.go_left(s - 1, rl.at[s - 1]).wait_recv()
-                rl[s - 1] = (rl[s - 1].astype(F32) + p[(z + NR - NEAR + s) % NR].astype(F32)).astype(BF)
-                self.go_left(s, rl.at[s - 1]).start()
+            for g in (1, -1):
+                self.one(g, s - 1).wait_recv()
+                t = self.odd[(1 - g) // 2, s - 1].astype(F32) + self.block(g, 2 * HOPS - 2 * s)[...].astype(F32)
+                if g > 0 or s > 1:
+                    self.two(g, s - 1).wait_recv()
+                    t = t + self.even[(1 - g) // 2, s - 1].astype(F32)
+                src = self.source(g, s)
+                src[...] = t.astype(BF)
+                self.two(g, s, src).start()
 
         def end(self):
-            self.go_right(FAR - 1, self.rr.at[FAR - 1]).wait_recv()
-            self.go_left(NEAR - 1, self.rl.at[NEAR - 1]).wait_recv()
+            t = self.p[z].astype(F32)
+            for g in (1, -1):
+                self.one(g, HOPS - 1).wait_recv()
+                self.two(g, HOPS - 1).wait_recv()
+                t = t + self.odd[(1 - g) // 2, HOPS - 1].astype(F32) + self.even[(1 - g) // 2, HOPS - 1].astype(F32)
 
             def drain():
-                for s in range(FAR):
-                    self.go_right(s, self.rr.at[s]).wait_send()
-                for s in range(NEAR):
-                    self.go_left(s, self.rl.at[s]).wait_send()
+                for s in range(HOPS):
+                    for g in (1, -1):
+                        self.one(g, s).wait_send()
+                        if g > 0 or s > 0:
+                            self.two(g, s).wait_send()
 
             drains.append(drain)
-            return self.p[z].astype(F32) + self.rr[FAR - 1].astype(F32) + self.rl[NEAR - 1].astype(F32)
+            return t
 
     class RingGather:
         def __init__(self, buf):
             self.buf = buf
-            self.r, self.l = take(FAR), take(NEAR)
-
-        def go_right(self, s):
-            b = self.buf.at[(z - s + NR) % NR]
-            return copy(b, b, self.r + s, right)
-
-        def go_left(self, s):
-            b = self.buf.at[(z + s) % NR]
-            return copy(b, b, self.l + s, left)
+            self.o = {g: take(HOPS) for g in (1, -1)}
+            self.e = {g: take(HOPS) for g in (1, -1)}
+
+        def one(self, g, s, frm):
+            b = self.buf.at[(z - g * frm + NR) % NR]
+            return copy(b, b, self.o[g] + s, ring[g])
+
+        def two(self, g, s, frm):
+            b = self.buf.at[(z - g * frm + NR) % NR]
+            return copy(b, b, self.e[g] + s, ring[2 * g])
 
         def step(self, s):
-            if s < FAR:
+            for g in (1, -1):
                 if s > 0:
-                    self.go_right(s - 1).wait_recv()
-                self.go_right(s).start()
-            if s < NEAR:
-                if s > 0:
-                    self.go_left(s - 1).wait_recv()
-                self.go_left(s).start()
+                    self.two(g, s - 1, 2 * s).wait_recv()
+                if g > 0 or s < HOPS - 1:
+                    self.two(g, s, 2 * s).start()
+                self.one(g, s, 2 * s).start()
 
         def end(self):
-            self.go_right(FAR - 1).wait_recv()
-            self.go_left(NEAR - 1).wait_recv()
+            self.two(1, HOPS - 1, 2 * HOPS).wait_recv()
+            for g in (1, -1):
+                for s in range(HOPS):
+                    self.one(g, s, 2 * s + 1).wait_recv()
 
             def drain():
-                for s in range(FAR):
-                    self.go_right(s).wait_send()
-                for s in range(NEAR):
-                    self.go_left(s).wait_send()
+                for g in (1, -1):
+                    for s in range(HOPS):
+                        self.one(g, s, 2 * s).wait_send()
+                        if g > 0 or s < HOPS - 1:
+                            self.two(g, s, 2 * s).wait_send()
 
             drains.append(drain)
 
@@ -331,18 +350,18 @@
     W[0, x] = wq_ref[...]
     gate = jnp.tanh(gate_ref[...])
     sp_b.load((up_ref[...].astype(F32) * gate).astype(BF))
-    im_z[z] = to_row(img_ref[...].astype(F32))
+    im_z[z] = jnp.zeros((1, 128), F32)
+    im_z[z, :, 0:TB] = img_ref[...].astype(F32)
     pl.semaphore_wait(barrier, NI - 1 + NX - 1 + NR - 1)
 
     sp_s.a()
     ex_lat.start()
     sp_b.a()
-    ex_wq.start()
     ex_iz.start()
     W[1, x] = wo_ref[...].T
-    ex_wo.start()
 
     sp_s.b()
+    ex_wq.start()
     ex_lat.wait()
     pick_r = lax.broadcasted_iota(jnp.int32, (LI, NI * 16), 0)
     pick_c = lax.broadcasted_iota(jnp.int32, (LI, NI * 16), 1)
@@ -352,9 +371,11 @@
         latc[s] = packed[:, s * 128 : (s + 1) * 128]
     latb[ja] = latc[ja]
     ex_l2.start()
+    sp_s.c()
     sp_b.b()
-    sp_s.c()
-    sp_b.c()
+    ex_iz.wait()
+    im_x[x] = im_z[...]
+    ex_ix.start()
 
     ex_l2.wait()
     lat = latb[...].reshape(NL, 128)
@@ -366,9 +387,8 @@
         for a in range(NA):
             kv_p[a % NX, a // NX, h] = part[a * LB : (a + 1) * LB]
     kv.a()
-    ex_iz.wait()
-    im_x[x] = im_z[...]
-    ex_ix.start()
+    sp_b.c()
+    ex_wo.start()
 
     def rows_times(rows, m, p):
         acc = dot(rows, W[m].reshape(DG, WD), 1, 0).astype(BF)
@@ -379,25 +399,20 @@
     ex_wq.wait()
     rows_times(strow[...], 0, q_p)
     q_s.step(0)
-    kv.b()
     sq = strow[...].astype(F32)
     sq = (sq * sq).astype(BF)
     e_p[...] = dot(jnp.ones((8, DG), BF), sq, 1, 1)[0:1]
     e_z.start()
+    kv.b()
     q_s.step(1)
+    for s in range(2, HOPS):
+        q_s.step(s)
+    kv.c()
     sp_b.d()
     ex_wo.wait()
     rows_times(brrow[...], 1, a_p)
-    q_s.step(2)
     a_s.step(0)
-    kv.c()
-    q_s.step(3)
-    a_s.step(1)
-    q_s.step(4)
-    a_s.step(2)
     kv.d()
-    q_s.step(5)
-    a_s.step(3)
     e_z.wait()
     energy = e_p[...]
     for k in range(1, NR):
@@ -416,12 +431,12 @@
     image = slot // LAT
     count = jnp.where(image == 0, cnt_ref[0], jnp.where(image == 1, cnt_ref[1], jnp.where(image == 2, cnt_ref[2], cnt_ref[3])))
     allowed = (image_col == image.astype(F32)) & (slot % LAT < count)
-    for s in range(6, FAR):
-        q_s.step(s)
-        a_s.step(s - 2)
-    kv.e()
     q = q_s.end() * inv_attn
     qs[...] = q.astype(BF)
+    a_s.step(1)
+    kv.e()
+    for s in range(2, HOPS - 1):
+        a_s.step(s)
     for h in range(HL):
         cols = slice(h * HS, (h + 1) * HS)
         sco = dot(qs[:, cols], kv.head(h), 1, 1) * scale
@@ -431,12 +446,10 @@
         probl[h] = pr.astype(BF)
         atrow[z, :, cols] = dot(probl[h], kv.head(HL + h), 1, 0).astype(BF)
     at_g.step(0)
-    for s in range(max(FAR - 2, 4), FAR):
-        a_s.step(s)
+    if HOPS > 2:
+        a_s.step(HOPS - 1)
     at_g.step(1)
-
     gs[...] = a_s.end().astype(BF)
-    at_g.step(2)
     inner = jnp.zeros((TB, 1), F32)
     for h in range(HL):
         cols = slice(h * HS, (h + 1) * HS)
@@ -459,14 +472,10 @@
     innr[ja, zh] = to_row(inner)
     in_g.start()
     lg.a()
-    at_g.step(3)
     qg_g.step(1)
-    at_g.step(4)
-    qg_g.step(2)
-    lg.b()
-    for s in range(5, FAR):
+    for s in range(2, HOPS):
         at_g.step(s)
-        qg_g.step(s - 2)
+        qg_g.step(s)
     at_g.end()
 
     def grad_parts(left_rows, right_rows, m):
@@ -481,16 +490,15 @@
 
     attn_rows = atrow[...].reshape(TG, WD)
     c_out.a(attn_rows, 1)
-    for s in range(max(FAR - 2, 3), FAR):
-        qg_g.step(s)
-    lg.c()
-    grad_parts(brrow[...], attn_rows, 1)
-    ex_go.start()
+    lg.b()
     in_g.wait()
     ex_in.start()
     qg_g.end()
     qg_rows = qgrow[...].reshape(TG, WD)
     c_norm.a(qg_rows, 0)
+    lg.c()
+    grad_parts(brrow[...], attn_rows, 1)
+    ex_go.start()
     c_out.b()
     grad_parts(strow[...], qg_rows, 0)
     ex_gq.start()
@@ -534,8 +542,8 @@
     ex_gj.start()
     for h in range(HL):
         cols = slice(h * HS, (h + 1) * HS)
-        gwk_ref[:, cols] = dot(latt[...], lg.head(h), 1, 0)
-        gwv_ref[:, cols] = dot(latt[...], lg.head(HL + h), 1, 0)
+        gwk_ref[:, cols] = dot(latt[...], lg.head(h), 1, 0).astype(BF)
+        gwv_ref[:, cols] = dot(latt[...], lg.head(HL + h), 1, 0).astype(BF)
     ex_gl.wait()
     t = gl[ia].astype(F32)
     for k in range(1, NI):
@@ -548,9 +556,9 @@
     ex_g2.start()
     gst_ref[...] = (up + c_norm.d()).astype(BF)
     ex_go.wait()
-    gwo_ref[...] = grad_sum(1).T
+    gwo_ref[...] = grad_sum(1).astype(BF)
     ex_gq.wait()
-    gwq_ref[...] = grad_sum(0)
+    gwq_ref[...] = grad_sum(0).astype(BF)
     ex_gj.wait()
     t = ggj[...]
     for k in range(1, NJ):
@@ -561,6 +569,12 @@
         glat_ref[:, s * 128 : (s + 1) * 128] = glf[s, 0:LR, :]
     for f in drains:
         f()
+
+
+def finish(*refs):
+    for i in range(8):
+        v = refs[i][...].astype(refs[8 + i].dtype)
+        refs[8 + i][...] = v.T if i == 6 else v
 
 
 def run(sizes, *args):
@@ -591,7 +605,7 @@
         ]
 
     def ringsum():
-        return [vm(BF, NR, TB, WD), vm(BF, NR // 2, TB, WD), vm(BF, NR - 1 - NR // 2, TB, WD), vm(BF, TB, WD)]
+        return [vm(BF, NR, TB, WD), vm(BF, 2, NR // 4, TB, WD), vm(BF, 2, NR // 4, TB, WD), vm(BF, TB, WD)]
 
     def collect():
         return [
@@ -616,14 +630,23 @@
     out = pl.pallas_call(
         functools.partial(kernel, sizes),
         out_shape=(
-            shape((TB, DL), BF), shape((TB, DL), BF), shape((LR, DL), BF), shape((WB, WD), F32),
-            shape((WB, WD), F32), shape((WB, WD), F32), shape((WD, WB), F32), shape((1, DL), F32),
+            shape((TB, DL), BF), shape((TB, DL), BF), shape((LR, DL), BF), shape((WB, WD), BF),
+            shape((WB, WD), BF), shape((WB, WD), BF), shape((WB, WD), BF), shape((1, DL), F32),
         ),
         in_specs=[v] * 8 + [s, v],
         out_specs=tuple([v] * 8),
         scratch_shapes=scratch,
         compiler_params=pltpu.CompilerParams(collective_id=0, has_side_effects=True, vmem_limit_bytes=56 * 2**20),
-    )(st, lat, wq, wk, wv, wo, gate.reshape(1, DL), img.reshape(TB, 1), cnt, up)
+    )(st, lat, wq, wk, wv, wo, gate.reshape(1, DL), img.reshape(1, TB), cnt, up)
+    out = pl.pallas_call(
+        finish,
+        out_shape=(
+            shape((TB, DL), BF), shape((TB, DL), BF), shape((LR, DL), BF), shape((WB, WD), F32),
+            shape((WB, WD), F32), shape((WB, WD), F32), shape((WD, WB), F32), shape((1, DL), F32),
+        ),
+        in_specs=[v] * 8,
+        out_specs=tuple([v] * 8),
+    )(*out)
     return (*out[:7], out[7].reshape(DL))
 
 

time: 161 us -> 156 us (0.969)
  local copies, waits for them, and re-layouts: 9.38 us -> 0 us
  Pallas kernels: 151 us -> 155 us
    unnamed x22 -> x0, local copies, waits for them, and re-layouts: 8.68 us -> none
    pallas_call x1, Pallas kernels: 151 us -> 153 us  [run(): pl.pallas_call(functools.partial(kernel, sizes), out_shape=(shape((TB, DL...]
    pallas_call x0 -> x1, Pallas kernels: none -> 2.23 us  [run(): pl.pallas_call(finish, out_shape=(shape((TB, DL), BF), shape((TB, DL), BF...]
where the time goes in v3:
time: 156 us
  Pallas kernels  155 us (99%)
    pallas_call x1, Pallas kernels, run(): pl.pallas_call(functools.partial(kernel, sizes), out_shape=(shape((TB, DL...  153 us

profile of v3, /device:TPU:1, one launch (start us, length us, event | category | flops | bytes accessed | tf_op | source)
XLA Modules:
  0.0 156.1 jit_solution(787249150142473454)
XLA Ops:
  0.6 153.2 %shard_map.161 = (bf16[32,1024]{1,0:T(8,128)(2,1)}, bf16[32,1024]{1,0:T(8,128)(2,1)}, bf16[4,1024]{1,0:T(4,128)(2,1)}, bf16[128,512]{1,0:T(8,128)(2,1)}, bf16[12...) custom-call(bf16[32,1024]{1,0:T(8,128)(2,1)} %refs_0_.1, ...), custom_call_target="tpu_custom_call" | custom-call | tf_op jit(solution)/shard_map/pallas_call | solution.py:630
  153.9 2.2 %shard_map.162 = (bf16[32,1024]{1,0:T(8,128)(2,1)}, bf16[32,1024]{1,0:T(8,128)(2,1)}, bf16[4,1024]{1,0:T(4,128)(2,1)}, f32[128,512]{1,0:T(8,128)}, f32[128,512]{...) custom-call(bf16[32,1024]{1,0:T(8,128)(2,1)} %get-tuple-element.24.refs_0_, ...), custom_call_target="tpu_custom_call" | custom-call | tf_op jit(solution)/shard_map/pallas_call | solution.py:641

commit v4 on v3

--- a/solution.py
+++ b/solution.py
@@ -64,7 +64,7 @@
     scale = 1.0 / math.sqrt(HS)
 
     ia, ja, al = lax.axis_index("ia"), lax.axis_index("ja"), lax.axis_index("al")
-    x, zh = al % NX, al // NX
+    x, zh = lax.rem(al, NX), lax.div(al, NX)
     z = zh * NJ + ja
     place = {"ia": (ia, NI), "ja": (ja, NJ), "x": (x, NX), "z": (z, NR)}
 
@@ -72,11 +72,19 @@
         if axis == "x":
             return {"al": zh * NX + i}
         if axis == "z":
-            return {"ja": i % NJ, "al": (i // NJ) * NX + x}
+            return {"ja": lax.rem(i, NJ), "al": lax.div(i, NJ) * NX + x}
         return {axis: i}
 
     used = [0]
     drains = []
+    seen = [0]
+
+    def settle():
+        for f in drains[: seen[0]]:
+            f()
+        del drains[: seen[0]]
+        seen[0] = len(drains)
+
 
     def take(n):
         used[0] += n
@@ -96,11 +104,11 @@
             self.base = take(self.n)
 
         def out(self, k):
-            peer = (self.me + k) % self.n
+            peer = lax.rem(self.me + k, self.n)
             return copy(self.src(peer), self.dst(self.me, k), self.base + k, device(self.axis, peer))
 
         def into(self, k):
-            peer = (self.me - k + self.n) % self.n
+            peer = lax.rem(self.me - k + self.n, self.n)
             return copy(self.src(peer), self.dst(peer, k), self.base + k, device(self.axis, peer))
 
         def start(self):
@@ -111,7 +119,7 @@
             loop(1, self.n, lambda k: self.into(k).wait_recv())
 
     HOPS = NR // 4
-    ring = {d: device("z", (z + d + NR) % NR) for d in (-2, -1, 1, 2)}
+    ring = {d: device("z", lax.rem(z + d + NR, NR)) for d in (-2, -1, 1, 2)}
 
     class RingSum:
         def __init__(self, p, odd, even):
@@ -120,7 +128,7 @@
             self.e = {g: take(HOPS) for g in (1, -1)}
 
         def block(self, g, off):
-            return self.p.at[(z + g * off + NR) % NR]
+            return self.p.at[lax.rem(z + g * off + NR, NR)]
 
         def one(self, g, i, src=None):
             dst = self.odd.at[(1 - g) // 2, i]
@@ -176,11 +184,11 @@
             self.e = {g: take(HOPS) for g in (1, -1)}
 
         def one(self, g, s, frm):
-            b = self.buf.at[(z - g * frm + NR) % NR]
+            b = self.buf.at[lax.rem(z - g * frm + NR, NR)]
             return copy(b, b, self.o[g] + s, ring[g])
 
         def two(self, g, s, frm):
-            b = self.buf.at[(z - g * frm + NR) % NR]
+            b = self.buf.at[lax.rem(z - g * frm + NR, NR)]
             return copy(b, b, self.e[g] + s, ring[2 * g])
 
         def step(self, s):
@@ -210,8 +218,8 @@
         def __init__(self, p, rx, zs, rz, full):
             self.p, self.rx, self.zs, self.rz, self.full = p, rx, zs, rz, full
             self.x1 = Exchange("x", lambda peer: p.at[peer], lambda s, k: rx.at[k])
-            self.z1 = Exchange("z", lambda peer: zs.at[peer // NJ, peer % NJ], lambda s, k: rz.at[k])
-            self.z2 = Exchange("z", lambda peer: full.at[x, zh, ja], lambda s, k: full.at[x, s // NJ, s % NJ])
+            self.z1 = Exchange("z", lambda peer: zs.at[lax.div(peer, NJ), lax.rem(peer, NJ)], lambda s, k: rz.at[k])
+            self.z2 = Exchange("z", lambda peer: full.at[x, zh, ja], lambda s, k: full.at[x, lax.div(s, NJ), lax.rem(s, NJ)])
             self.x2 = Exchange("x", lambda peer: full.at[x], lambda s, k: full.at[s])
 
         def a(self):
@@ -246,7 +254,7 @@
     class Spread:
         def __init__(self, t0, t1, t2, t3, rows):
             self.t0, self.t1, self.t2, self.t3, self.rows = t0, t1, t2, t3, rows
-            self.z = Exchange("ja", lambda peer: t0.at[peer], lambda s, k: t1.at[s // NZ, s % NZ])
+            self.z = Exchange("ja", lambda peer: t0.at[peer], lambda s, k: t1.at[lax.div(s, NZ), lax.rem(s, NZ)])
             self.x = Exchange("x", lambda peer: t1.at[peer], lambda s, k: t2.at[s])
             self.y = Exchange("ia", lambda peer: t3.at[ia], lambda s, k: t3.at[s])
 
@@ -279,7 +287,7 @@
             self.p, self.r, self.t1, self.t2, self.t3 = p, r, t1, t2, t3
             self.y = Exchange("ia", lambda peer: p.at[peer], lambda s, k: r.at[k])
             self.x = Exchange("x", lambda peer: t1.at[peer], lambda s, k: t2.at[s])
-            self.z = Exchange("ja", lambda peer: t2.at[peer // NZ, peer % NZ], lambda s, k: t3.at[s])
+            self.z = Exchange("ja", lambda peer: t2.at[lax.div(peer, NZ), lax.rem(peer, NZ)], lambda s, k: t3.at[s])
 
         def a(self, rows, m):
             for k in range(NX):
@@ -320,7 +328,7 @@
     ex_iz = Exchange("z", lambda peer: im_z.at[z], lambda s, k: im_z.at[s])
     ex_ix = Exchange("x", lambda peer: im_x.at[x], lambda s, k: im_x.at[s])
     at_g, qg_g = RingGather(atrow), RingGather(qgrow)
-    in_g = Exchange("z", lambda peer: innr.at[ja, zh], lambda s, k: innr.at[s % NJ, s // NJ])
+    in_g = Exchange("z", lambda peer: innr.at[ja, zh], lambda s, k: innr.at[lax.rem(s, NJ), lax.div(s, NJ)])
     ex_in = Exchange("ia", lambda peer: innr.at[peer], lambda s, k: rin.at[k])
     c_out, c_norm = Collect(outp, outr, out1, out2, out3), Collect(normp, normr, norm1, norm2, norm3)
     ex_gi = Exchange("ia", lambda peer: gg_p, lambda s, k: gg_r.at[k])
@@ -333,7 +341,7 @@
     barrier = pltpu.get_barrier_semaphore()
     for axis in ("ia", "x", "z"):
         i, n = place[axis]
-        loop(1, n, lambda k: pl.semaphore_signal(barrier, 1, device_id=device(axis, (i + k) % n), device_id_type=MESH))
+        loop(1, n, lambda k: pl.semaphore_signal(barrier, 1, device_id=device(axis, lax.rem(i + k, n)), device_id_type=MESH))
 
     lane1 = lax.broadcasted_iota(jnp.int32, (TB, 128), 1)
     sub1 = lax.broadcasted_iota(jnp.int32, (TB, 128), 0)
@@ -377,6 +385,7 @@
     im_x[x] = im_z[...]
     ex_ix.start()
 
+    settle()
     ex_l2.wait()
     lat = latb[...].reshape(NL, 128)
     latt[...] = lat.T
@@ -395,6 +404,7 @@
         for d in range(NR):
             p[d] = acc[d * TB : (d + 1) * TB]
 
+    settle()
     sp_s.d()
     ex_wq.wait()
     rows_times(strow[...], 0, q_p)
@@ -404,14 +414,18 @@
     e_p[...] = dot(jnp.ones((8, DG), BF), sq, 1, 1)[0:1]
     e_z.start()
     kv.b()
-    q_s.step(1)
-    for s in range(2, HOPS):
-        q_s.step(s)
-    kv.c()
+    settle()
     sp_b.d()
     ex_wo.wait()
     rows_times(brrow[...], 1, a_p)
     a_s.step(0)
+    q_s.step(1)
+    a_s.step(1)
+    kv.c()
+    for s in range(2, HOPS):
+        settle()
+        q_s.step(s)
+        a_s.step(s)
     kv.d()
     e_z.wait()
     energy = e_p[...]
@@ -433,10 +447,9 @@
     allowed = (image_col == image.astype(F32)) & (slot % LAT < count)
     q = q_s.end() * inv_attn
     qs[...] = q.astype(BF)
-    a_s.step(1)
+    gs[...] = a_s.end().astype(BF)
+    settle()
     kv.e()
-    for s in range(2, HOPS - 1):
-        a_s.step(s)
     for h in range(HL):
         cols = slice(h * HS, (h + 1) * HS)
         sco = dot(qs[:, cols], kv.head(h), 1, 1) * scale
@@ -446,10 +459,6 @@
         probl[h] = pr.astype(BF)
         atrow[z, :, cols] = dot(probl[h], kv.head(HL + h), 1, 0).astype(BF)
     at_g.step(0)
-    if HOPS > 2:
-        a_s.step(HOPS - 1)
-    at_g.step(1)
-    gs[...] = a_s.end().astype(BF)
     inner = jnp.zeros((TB, 1), F32)
     for h in range(HL):
         cols = slice(h * HS, (h + 1) * HS)
@@ -469,14 +478,16 @@
             lg_p[a % NX, a // NX, h] = kt[a * LB : (a + 1) * LB]
             lg_p[a % NX, a // NX, HL + h] = vt[a * LB : (a + 1) * LB]
     qg_g.step(0)
+    lg.a()
     innr[ja, zh] = to_row(inner)
     in_g.start()
-    lg.a()
+    at_g.step(1)
     qg_g.step(1)
+    lg.b()
     for s in range(2, HOPS):
+        settle()
         at_g.step(s)
         qg_g.step(s)
-    at_g.end()
 
     def grad_parts(left_rows, right_rows, m):
         for k in range(NX):
@@ -488,22 +499,21 @@
             t = t + gpr[m, k].astype(F32)
         return t
 
+    at_g.end()
     attn_rows = atrow[...].reshape(TG, WD)
     c_out.a(attn_rows, 1)
-    lg.b()
-    in_g.wait()
-    ex_in.start()
     qg_g.end()
     qg_rows = qgrow[...].reshape(TG, WD)
     c_norm.a(qg_rows, 0)
     lg.c()
+    in_g.wait()
+    ex_in.start()
     grad_parts(brrow[...], attn_rows, 1)
     ex_go.start()
+    settle()
     c_out.b()
     grad_parts(strow[...], qg_rows, 0)
     ex_gq.start()
-    lg.d()
-    c_out.c()
 
     def correct(t):
         ex_in.wait()
@@ -517,12 +527,16 @@
         return jnp.stack(parts, axis=1)
 
     c_norm.b(correct)
+    c_out.c()
+    lg.d()
+    settle()
+    c_norm.c()
     up = up_ref[...].astype(F32)
     branch = c_out.d()
     mixed_ref[...] = (st_ref[...].astype(F32) + gate * branch).astype(BF)
     gg_p[...] = jnp.sum(up * branch * (1.0 - gate * gate), axis=0, keepdims=True)
     ex_gi.start()
-    c_norm.c()
+    settle()
     lg.e()
     total = jnp.zeros((NL, 128), F32)
     for h in range(HL):
@@ -534,16 +548,17 @@
     perm = (coli == from_row).astype(F32).astype(BF)
     gl[...] = dot(perm, total.astype(BF), 1, 0).astype(BF).reshape(NI, NJ * LR, 128)
     ex_gl.start()
+    for h in range(HL):
+        cols = slice(h * HS, (h + 1) * HS)
+        gwk_ref[:, cols] = dot(latt[...], lg.head(h), 1, 0).astype(BF)
+        gwv_ref[:, cols] = dot(latt[...], lg.head(HL + h), 1, 0).astype(BF)
     ex_gi.wait()
     t = gg_p[...]
     for k in range(1, NI):
         t = t + gg_r[k]
     ggj[...] = t
     ex_gj.start()
-    for h in range(HL):
-        cols = slice(h * HS, (h + 1) * HS)
-        gwk_ref[:, cols] = dot(latt[...], lg.head(h), 1, 0).astype(BF)
-        gwv_ref[:, cols] = dot(latt[...], lg.head(HL + h), 1, 0).astype(BF)
+    settle()
     ex_gl.wait()
     t = gl[ia].astype(F32)
     for k in range(1, NI):
@@ -555,6 +570,7 @@
     glf[ja] = gls[ja]
     ex_g2.start()
     gst_ref[...] = (up + c_norm.d()).astype(BF)
+    settle()
     ex_go.wait()
     gwo_ref[...] = grad_sum(1).astype(BF)
     ex_gq.wait()

time: 156 us -> 146 us (0.936)
  Pallas kernels: 155 us -> 146 us
    pallas_call x1, Pallas kernels: 153 us -> 143 us  [run(): pl.pallas_call(functools.partial(kernel, sizes), out_shape=(shape((TB, DL...]
where the time goes in v4:
time: 146 us
  Pallas kernels  146 us (100%)
    pallas_call x1, Pallas kernels, run(): pl.pallas_call(functools.partial(kernel, sizes), out_shape=(shape((TB, DL...  143 us

profile of v4, /device:TPU:1, one launch (start us, length us, event | category | flops | bytes accessed | tf_op | source)
XLA Modules:
  0.0 146.3 jit_solution(15990084047533280951)
XLA Ops:
  0.6 143.4 %shard_map.161 = (bf16[32,1024]{1,0:T(8,128)(2,1)}, bf16[32,1024]{1,0:T(8,128)(2,1)}, bf16[4,1024]{1,0:T(4,128)(2,1)}, bf16[128,512]{1,0:T(8,128)(2,1)}, bf16[12...) custom-call(bf16[32,1024]{1,0:T(8,128)(2,1)} %refs_0_.1, ...), custom_call_target="tpu_custom_call" | custom-call | tf_op jit(solution)/shard_map/pallas_call | solution.py:646
  144.0 2.2 %shard_map.162 = (bf16[32,1024]{1,0:T(8,128)(2,1)}, bf16[32,1024]{1,0:T(8,128)(2,1)}, bf16[4,1024]{1,0:T(4,128)(2,1)}, f32[128,512]{1,0:T(8,128)}, f32[128,512]{...) custom-call(bf16[32,1024]{1,0:T(8,128)(2,1)} %get-tuple-element.24.refs_0_, ...), custom_call_target="tpu_custom_call" | custom-call | tf_op jit(solution)/shard_map/pallas_call | solution.py:657

commit v5 on v4

--- a/solution.py
+++ b/solution.py
@@ -365,11 +365,11 @@
     sp_s.a()
     ex_lat.start()
     sp_b.a()
-    ex_iz.start()
     W[1, x] = wo_ref[...].T
 
     sp_s.b()
     ex_wq.start()
+    ex_iz.start()
     ex_lat.wait()
     pick_r = lax.broadcasted_iota(jnp.int32, (LI, NI * 16), 0)
     pick_c = lax.broadcasted_iota(jnp.int32, (LI, NI * 16), 1)
@@ -395,8 +395,8 @@
         part = dot(lat, wref[:, c * HS : (c + 1) * HS], 1, 0).astype(BF)
         for a in range(NA):
             kv_p[a % NX, a // NX, h] = part[a * LB : (a + 1) * LB]
+    sp_b.c()
     kv.a()
-    sp_b.c()
     ex_wo.start()
 
     def rows_times(rows, m, p):

time: 146 us -> 146 us (level)
  no operation moved by 1% of the time
where the time goes in v5:
time: 146 us
  Pallas kernels  145 us (99%)
    pallas_call x1, Pallas kernels, run(): pl.pallas_call(functools.partial(kernel, sizes), out_shape=(shape((TB, DL...  143 us

profile of v5, /device:TPU:1, one launch (start us, length us, event | category | flops | bytes accessed | tf_op | source)
XLA Modules:
  0.0 146.0 jit_solution(3228148187001182130)
XLA Ops:
  0.6 143.1 %shard_map.161 = (bf16[32,1024]{1,0:T(8,128)(2,1)}, bf16[32,1024]{1,0:T(8,128)(2,1)}, bf16[4,1024]{1,0:T(4,128)(2,1)}, bf16[128,512]{1,0:T(8,128)(2,1)}, bf16[12...) custom-call(bf16[32,1024]{1,0:T(8,128)(2,1)} %refs_0_.1, ...), custom_call_target="tpu_custom_call" | custom-call | tf_op jit(solution)/shard_map/pallas_call | solution.py:646
  143.8 2.2 %shard_map.162 = (bf16[32,1024]{1,0:T(8,128)(2,1)}, bf16[32,1024]{1,0:T(8,128)(2,1)}, bf16[4,1024]{1,0:T(4,128)(2,1)}, f32[128,512]{1,0:T(8,128)}, f32[128,512]{...) custom-call(bf16[32,1024]{1,0:T(8,128)(2,1)} %get-tuple-element.24.refs_0_, ...), custom_call_target="tpu_custom_call" | custom-call | tf_op jit(solution)/shard_map/pallas_call | solution.py:657
